TPU v7x, 256 devices: a whole 4x4x8 slice. The times are simulated.
256 devices in a mesh: ctx: 32 (over x, z_lo, y), head: 8 (over z_hi, core).
Axes of the slice: x: 4, y: 4, z: 8 (z_hi: 4, z_lo: 2; z = z_hi * 2 + z_lo), core: 2. Of those that a mesh axis runs over, the one named last changes fastest.
Arguments:
- queries: bfloat16 [8192, 56, 128], P('ctx', 'head'), may hold values from -6 to 6
- keys: bfloat16 [8192, 8, 128], P('ctx', 'head'), may hold values from -6 to 6
- values: bfloat16 [8192, 8, 128], P('ctx', 'head'), may hold values from -6 to 6
- out_weight: bfloat16 [7168, 3584], P('head'), may hold values from -0.0625 to 0.0625
- segment_info: int32 [64, 3], replicated, may hold values from 0 to 8192, as said below
- block_order: int32 [64], replicated, may hold values from 0 to 63, each once
Outputs:
- projected: bfloat16 [8192, 3584], P(('ctx', 'head'))
Inputs may be any that keep to these rules, and one draw needn't show every extreme that they name: `segment_info`: segments are runs of 1 to 4 whole prompt blocks that cover the prompt in order; all blocks of a segment have equal rows; the first segment is causal.
All inputs are finite; a program needn't handle non-finite values.
Results may differ from a plain program's by a relative error of at most 0.02.
Values may be sent and summed in bfloat16 or wider, within the bound.
No kernel may reach another device: no remote copies, remote signals or barrier semaphores. Data moves between devices by JAX's collectives and lax.ppermute only.
A program may use at most 64 MiB of HBM per device.

v0:
```python
import functools
import math

import jax
import jax.numpy as jnp
from jax import lax
from jax.experimental import pallas as pl
from jax.experimental.pallas import tpu as pltpu
from jax.sharding import Mesh, PartitionSpec as P

BLK = 128
HD = 128
GROUP = 7
ROWS = 256
FEATS = GROUP * HD
BLOCKS = 64
CHUNK = 16
MINUS = -1e30
SIZES = {"x": 4, "zl": 2, "y": 4, "zh": 4, "core": 2}
AXES = tuple(SIZES)
CTX = ("x", "zl", "y")
HEAD = ("zh", "core")
OFFSETS = (0, -1, 1, 2)
SMEM = pl.BlockSpec(memory_space=pltpu.SMEM)
VMEM = pl.BlockSpec(memory_space=pltpu.VMEM)
ANYWHERE = pl.BlockSpec(memory_space=pl.ANY)


def shift(value, axis, step):
    size = SIZES[axis]
    return lax.ppermute(value, axis, [((i + step) % size, i) for i in range(size)])


def ring_index(there, here):
    off = (there - here) & 3
    return jnp.where(off == 0, 0, jnp.where(off == 3, 1, jnp.where(off == 1, 2, 3)))


def table_kernel(order_ref, where_ref, table_ref, inv_ref):
    my_x, my_zl, my_y = where_ref[0], where_ref[1], where_ref[2]

    def invert(block, _):
        inv_ref[order_ref[block]] = block
        table_ref[block] = 0
        table_ref[BLOCKS + block] = BLOCKS
        return 0

    lax.fori_loop(0, BLOCKS, invert, 0)

    def place(position, count):
        block = inv_ref[position]
        ctx = block >> 1
        x_part = ring_index(ctx >> 3, my_x)
        y_part = ring_index(ctx & 3, my_y)
        even = (block & 1) == 0
        here = ((ctx >> 2) & 1) == my_zl

        @pl.when(here)
        def _():
            table_ref[count] = jnp.where(even, x_part * 4 + y_part, 16 + y_part * 4 + x_part)
            table_ref[BLOCKS + count] = position

        count = count + here.astype(jnp.int32)
        table_ref[2 * BLOCKS + position] = count
        return count

    lax.fori_loop(0, BLOCKS, place, jnp.int32(0))


def make_table(order, where):
    return pl.pallas_call(
        table_kernel,
        out_shape=jax.ShapeDtypeStruct((3 * BLOCKS,), jnp.int32),
        in_specs=[SMEM, SMEM],
        out_specs=SMEM,
        scratch_shapes=[pltpu.SMEM((BLOCKS,), jnp.int32)],
        name="table",
    )(order, where)


def attend_kernel(flip, order_ref, info_ref, where_ref, table_ref, q_ref, *refs):
    parts = refs[:8]
    out_ref, kv_ref, qs_ref, m_ref, l_ref, acc_ref, kv_sem = refs[8:]
    part_rows = parts[0].shape[0]
    copies = [
        pltpu.make_async_copy(part, kv_ref.at[pl.ds(i * part_rows, part_rows)], kv_sem.at[i])
        for i, part in enumerate(parts)
    ]
    for copy in copies:
        copy.start()
    my_x, my_zl, my_y = where_ref[0], where_ref[1], where_ref[2]
    first_block = ((my_x * 2 + (my_zl ^ flip)) * 4 + my_y) * 2
    scale = math.log2(math.e) / math.sqrt(HD)
    rows = GROUP * BLK
    for copy in copies:
        copy.wait()

    def one_block(t, _):
        block = order_ref[first_block + t]
        last = info_ref[block * 3 + 1]
        kind = info_ref[block * 3 + 2]
        most_block = jnp.where(kind == 1, lax.div(last, BLK) - 1, block)
        count = table_ref[2 * BLOCKS + most_block]
        q_rows = pl.ds(pl.multiple_of(t * BLK, BLK), BLK)
        for h in range(GROUP):
            scaled = q_ref[h, q_rows, :].astype(jnp.float32) * scale
            high = scaled.astype(jnp.bfloat16)
            qs_ref[h * BLK : (h + 1) * BLK, 0:HD] = high
            qs_ref[h * BLK : (h + 1) * BLK, HD:] = (scaled - high.astype(jnp.float32)).astype(jnp.bfloat16)
        m_ref[...] = jnp.full_like(m_ref, MINUS)
        l_ref[...] = jnp.zeros_like(l_ref)
        acc_ref[...] = jnp.zeros_like(acc_ref)

        def step(begin, size, masked):
            key_list, value_list = [], []
            for j in range(size):
                start = pl.multiple_of(table_ref[begin + j] * (2 * BLK), 2 * BLK)
                key_list.append(kv_ref[pl.ds(start, BLK), :])
                value_list.append(kv_ref[pl.ds(start + BLK, BLK), :])
            key_tile = jnp.concatenate(key_list, axis=0)
            value_tile = jnp.concatenate(value_list, axis=0)
            twice = jnp.concatenate([key_tile, key_tile], axis=1)
            s = lax.dot_general(
                qs_ref[...], twice, (((1,), (1,)), ((), ())), preferred_element_type=jnp.float32
            )
            if masked:
                lane = lax.broadcasted_iota(jnp.int32, (rows, BLK), 1)
                row = lax.broadcasted_iota(jnp.int32, (rows, BLK), 0) & (BLK - 1)
                most = jnp.where(kind == 1, last - 1, block * BLK + row) - lane
                s = jnp.concatenate(
                    [
                        jnp.where(
                            table_ref[BLOCKS + begin + j] * BLK <= most, s[:, j * BLK : (j + 1) * BLK], MINUS
                        )
                        for j in range(size)
                    ],
                    axis=1,
                )
            m_old = m_ref[...]
            m_new = jnp.maximum(m_old, jnp.max(s, axis=1, keepdims=True))
            p = jnp.exp2(s - jnp.concatenate([m_new] * size, axis=1))
            fade = jnp.exp2(m_old - m_new)
            l_ref[...] = l_ref[...] * fade + sum(p[:, i * BLK : (i + 1) * BLK] for i in range(size))
            m_ref[...] = m_new
            acc_ref[...] = acc_ref[...] * fade + jnp.dot(
                p.astype(jnp.bfloat16), value_tile, preferred_element_type=jnp.float32
            )

        full = lax.div(jnp.maximum(count - 1, 0), CHUNK)

        def full_step(chunk, _):
            step(chunk * CHUNK, CHUNK, False)
            return 0

        lax.fori_loop(0, full, full_step, 0)
        rest = count - full * CHUNK
        for size in (4, 8, 12, 16):

            @pl.when((rest > size - 4) & (rest <= size))
            def _(size=size):
                step(full * CHUNK, size, True)

        lane = lax.broadcasted_iota(jnp.int32, (BLK, BLK), 1)
        stats = jnp.zeros((BLK, BLK), jnp.float32)
        for h in range(GROUP):
            part = slice(h * BLK, (h + 1) * BLK)
            total = jnp.sum(l_ref[part, :], axis=1, keepdims=True)
            safe = jnp.where(total > 0, total, 1.0)
            out_ref[q_rows, h * HD : (h + 1) * HD] = (acc_ref[part, :] / safe).astype(jnp.bfloat16)
            level = m_ref[part, :] + jnp.log2(safe)
            high = level.astype(jnp.bfloat16).astype(jnp.float32)
            middle = (level - high).astype(jnp.bfloat16).astype(jnp.float32)
            stats = jnp.where(lane == h, high, stats)
            stats = jnp.where(lane == 8 + h, middle, stats)
            stats = jnp.where(lane == 16 + h, level - high - middle, stats)
        out_ref[q_rows, FEATS:] = stats.astype(jnp.bfloat16)
        return 0

    lax.fori_loop(0, 2, one_block, 0)


def attend(flip, order, info, where, table, q, parts):
    part_rows = parts[0].shape[0]
    rows = GROUP * BLK
    return pl.pallas_call(
        functools.partial(attend_kernel, flip),
        out_shape=jax.ShapeDtypeStruct((ROWS, FEATS + BLK), jnp.bfloat16),
        in_specs=[SMEM, SMEM, SMEM, SMEM, VMEM] + [ANYWHERE] * 8,
        out_specs=VMEM,
        scratch_shapes=[
            pltpu.VMEM((8 * part_rows, HD), jnp.bfloat16),
            pltpu.VMEM((rows, 2 * HD), jnp.bfloat16),
            pltpu.VMEM((rows, BLK), jnp.float32),
            pltpu.VMEM((rows, BLK), jnp.float32),
            pltpu.VMEM((rows, HD), jnp.float32),
            pltpu.SemaphoreType.DMA((8,)),
        ],
        compiler_params=pltpu.CompilerParams(vmem_limit_bytes=40 * 1024 * 1024),
        cost_estimate=pl.CostEstimate(flops=4_000_000_000, bytes_accessed=3_000_000, transcendentals=4_000_000),
        name="attend",
    )(order, info, where, table, q, *parts)


def project_kernel(where_ref, a_ref, b_ref, w_ref, keep_ref, send_ref, att_ref):
    my_zh, my_core = where_ref[3], where_ref[4]

    @pl.when(pl.program_id(0) == 0)
    def _():
        stats_a = a_ref[:, FEATS:].astype(jnp.float32)
        stats_b = b_ref[:, FEATS:].astype(jnp.float32)
        for h in range(GROUP):

            def level(stats):
                return stats[:, h : h + 1] + stats[:, 8 + h : 9 + h] + stats[:, 16 + h : 17 + h]

            weight_a = 1.0 / (1.0 + jnp.exp2(level(stats_b) - level(stats_a)))
            cols = slice(h * HD, (h + 1) * HD)
            a, b = a_ref[:, cols].astype(jnp.float32), b_ref[:, cols].astype(jnp.float32)
            att_ref[:, cols] = (b + (a - b) * weight_a).astype(jnp.bfloat16)

    res = jnp.dot(att_ref[...], w_ref[...], preferred_element_type=jnp.float32).astype(jnp.bfloat16)
    for z in range(4):
        to = (z - my_zh) & 3
        zero, one = res[z * 64 : z * 64 + 32, :], res[z * 64 + 32 : z * 64 + 64, :]
        keep_ref[to] = jnp.where(my_core == 0, zero, one)
        send_ref[to] = jnp.where(my_core == 0, one, zero)


def project(where, a, b, w):
    out_cols = w.shape[1]
    tile = 512
    piece = jax.ShapeDtypeStruct((4, 32, out_cols), jnp.bfloat16)
    out_spec = pl.BlockSpec((4, 32, tile), lambda i: (0, 0, i))
    return pl.pallas_call(
        project_kernel,
        grid=(out_cols // tile,),
        out_shape=(piece, piece),
        in_specs=[
            SMEM,
            pl.BlockSpec(a.shape, lambda i: (0, 0)),
            pl.BlockSpec(b.shape, lambda i: (0, 0)),
            pl.BlockSpec((w.shape[0], tile), lambda i: (0, i)),
        ],
        out_specs=(out_spec, out_spec),
        scratch_shapes=[pltpu.VMEM((ROWS, FEATS), jnp.bfloat16)],
        compiler_params=pltpu.CompilerParams(vmem_limit_bytes=24 * 1024 * 1024),
        cost_estimate=pl.CostEstimate(flops=1_640_000_000, bytes_accessed=9_000_000, transcendentals=1792),
        name="project",
    )(where, a, b, w)


def body(queries, keys, values, out_weight, segment_info, block_order):
    where = jnp.stack([lax.axis_index(axis) for axis in AXES]).astype(jnp.int32)
    info = segment_info.reshape(-1)
    k, v = keys[:, 0, :], values[:, 0, :]
    q = jnp.transpose(queries, (1, 0, 2))
    first = jnp.concatenate([k[:BLK], v[:BLK]], axis=0)
    second = jnp.concatenate([k[BLK:], v[BLK:]], axis=0)
    first = jnp.concatenate([first] + [shift(first, "y", o) for o in OFFSETS[1:]], axis=0)
    second = jnp.concatenate([second] + [shift(second, "x", o) for o in OFFSETS[1:]], axis=0)
    parts = [first] + [shift(first, "x", o) for o in OFFSETS[1:]]
    parts += [second] + [shift(second, "y", o) for o in OFFSETS[1:]]
    other_q = shift(q, "zl", 1)
    table = make_table(block_order, where)
    other = attend(1, block_order, info, where, table, other_q, parts)
    back = shift(other, "zl", 1)
    own = attend(0, block_order, info, where, table, q, parts)
    keep, send = project(where, own, back, out_weight)
    pieces = keep.astype(jnp.float32) + shift(send, "core", 1).astype(jnp.float32)
    low = pieces.astype(jnp.bfloat16)
    total = pieces[0]
    for j in (1, 3, 2):
        total = total + shift(low[j], "zh", -j).astype(jnp.float32)
    return total.astype(jnp.bfloat16)


def solution(mesh):
    fine = Mesh(mesh.devices.reshape(tuple(SIZES.values())), AXES)
    placed = (
        P(CTX, HEAD, None),
        P(CTX, HEAD, None),
        P(CTX, HEAD, None),
        P(HEAD, None),
        P(),
        P(),
    )
    return jax.shard_map(body, mesh=fine, in_specs=placed, out_specs=P(AXES, None), check_vma=False)
```

profile of v0, /device:TPU:1, one launch (start us, length us, event | category | flops | bytes accessed | tf_op | source)
XLA Modules:
  0.0 98.0 jit_solution(5045123510520502084)
XLA Ops:
  0.0 0.8 slice_bitcast_fusion.4
  0.8 3.8 %collective-permute-start.2 = (bf16[256,128]{1,0:T(8,128)(2,1)S(1)}, bf16[256,128]{1,0:T(8,128)(2,1)S(1)}, u32[]{:S(2)}, u32[]{:S(2)}) collective-permute-start(bf16[256,128]{1,0:T(8,128)(2,1)S(1)} %pad_maximum_fusion), channel_id=1, source_target_pairs={{16,0},{24,8},{0,16},{8,24},{17,1},{25,9},{1,17},{9,25},{18,2},{26... | collective-permute-start | bytes 196616 | tf_op jit(solution)/shard_map/ppermute | solution.py:31
  4.7 0.8 collective-permute-start.1
  5.4 0.7 collective-permute-start
  6.1 2.7 %collective-permute-start.8 = (bf16[256,128]{1,0:T(8,128)(2,1)S(1)}, bf16[256,128]{1,0:T(8,128)(2,1)S(1)}, u32[]{:S(2)}, u32[]{:S(2)}) collective-permute-start(bf16[256,128]{1,0:T(8,128)(2,1)S(1)} %pad_maximum_fusion.1), channel_id=1, source_target_pairs={{128,0},{192,64},{0,128},{64,192},{129,1},{193,65},{1,129},{65,193... | collective-permute-start | bytes 196616 | tf_op jit(solution)/shard_map/ppermute | solution.py:31
  8.9 0.9 collective-permute-start.7
  9.7 0.8 constant_dynamic-update-slice_fusion.9
  10.5 0.8 constant_dynamic-update-slice_fusion.8
  12.0 1.7 %collective-permute-start.12 = (bf16[7,256,128]{2,1,0:T(8,128)(2,1)}, bf16[7,256,128]{2,1,0:T(8,128)(2,1)S(1)}, u32[]{:S(2)}, u32[]{:S(2)}) collective-permute-start(bf16[7,256,128]{2,1,0:T(8,128)(2,1)} %bitcast.40), channel_id=1, source_target_pairs={{32,0},{0,32},{33,1},{1,33},{34,2},{2,34},{35,3},{3,35},{36,4},{4,... | collective-permute-start | bytes 1376264 | tf_op jit(solution)/shard_map/ppermute | solution.py:31
  13.8 1.5 %collective-permute-start.5 = (bf16[1024,128]{1,0:T(8,128)(2,1)S(1)}, bf16[1024,128]{1,0:T(8,128)(2,1)S(1)}, u32[]{:S(2)}, u32[]{:S(2)}) collective-permute-start(bf16[1024,128]{1,0:T(8,128)(2,1)S(1)} %constant_dynamic-update-slice_fusion.refs_0_), channel_id=1, source_target_pairs={{128,0},{192,64},{0,128},{64,192},{129,1},{193,65},{1,129},{65,193... | collective-permute-start | bytes 786440 | tf_op jit(solution)/shard_map/ppermute | solution.py:31
  15.7 0.9 collective-permute-start.4
  17.3 0.9 collective-permute-start.11
  18.2 2.6 %collective-permute-done.5.refs_3_ = bf16[1024,128]{1,0:T(8,128)(2,1)S(1)} collective-permute-done((bf16[1024,128]{1,0:T(8,128)(2,1)S(1)}, bf16[1024,128]{1,0:T(8,128)(2,1)S(1)}, u32[]{:S(2)}, u32[]{:S(2)}) %collective-permute-start.5) | collective-permute-done | bytes 262176 | tf_op jit(solution)/shard_map/ppermute | solution.py:31
  20.8 1.9 %collective-permute-start.10 = (bf16[1024,128]{1,0:T(8,128)(2,1)S(1)}, bf16[1024,128]{1,0:T(8,128)(2,1)S(1)}, u32[]{:S(2)}, u32[]{:S(2)}) collective-permute-start(bf16[1024,128]{1,0:T(8,128)(2,1)S(1)} %constant_dynamic-update-slice_fusion.5.refs_4_), channel_id=1, source_target_pairs={{8,0},{16,8},{24,16},{0,24},{9,1},{17,9},{25,17},{1,25},{10,2},{18... | collective-permute-start | bytes 786440 | tf_op jit(solution)/shard_map/ppermute | solution.py:31
  22.7 3.2 %collective-permute-done.4.refs_2_ = bf16[1024,128]{1,0:T(8,128)(2,1)S(1)} collective-permute-done((bf16[1024,128]{1,0:T(8,128)(2,1)S(1)}, bf16[1024,128]{1,0:T(8,128)(2,1)S(1)}, u32[]{:S(2)}, u32[]{:S(2)}) %collective-permute-start.4) | collective-permute-done | bytes 262176 | tf_op jit(solution)/shard_map/ppermute | solution.py:31
  26.3 0.8 copy.7
  27.9 2.9 %table.1.table_ref = s32[192]{0:T(256)} custom-call(s32[64]{0:T(128)} %order_ref.5, s32[5]{0:T(128)} %stack.23.where_ref), custom_call_target="tpu_custom_call" | custom-call | tf_op jit(solution)/shard_map/table/pallas_call | solution.py:71
  30.9 4.9 %collective-permute-done.9.refs_5_ = bf16[1024,128]{1,0:T(8,128)(2,1)S(1)} collective-permute-done((bf16[1024,128]{1,0:T(8,128)(2,1)S(1)}, bf16[1024,128]{1,0:T(8,128)(2,1)S(1)}, u32[]{:S(2)}, u32[]{:S(2)}) %collective-permute-start.9) | collective-permute-done | bytes 262176 | tf_op jit(solution)/shard_map/ppermute | solution.py:31
  37.8 5.9 %attend.3 = bf16[256,1024]{1,0:T(8,128)(2,1)S(1)} custom-call(s32[64]{0:T(128)S(1)} %copy-done.3, s32[192]{0:T(256)S(1)} %reshape.7.info_ref, s32[5]{0:T(128)S(1)} %copy-done, s32[192]{0:T(256)S(1)} %copy-done.1, bf16[7,256,128]{2,1,0:T(8,128)(2,1)S(1)} %collective-permute-done.12.q_ref, bf16[1024,128]{1,0:T(8,128)(2,1)S(1)} %constant_dynamic-update-slice_fusion.refs_0_, ...), custom_call_target="tpu_custom_call" | custom-call | flops 4000000000 | bytes 3000000 | tf_op jit(solution)/shard_map/attend/pallas_call | solution.py:185
  43.7 2.8 %collective-permute-start.13 = (bf16[256,1024]{1,0:T(8,128)(2,1)S(1)}, bf16[256,1024]{1,0:T(8,128)(2,1)S(1)}, u32[]{:S(2)}, u32[]{:S(2)}) collective-permute-start(bf16[256,1024]{1,0:T(8,128)(2,1)S(1)} %attend.3), channel_id=1, source_target_pairs={{32,0},{0,32},{33,1},{1,33},{34,2},{2,34},{35,3},{3,35},{36,4},{4,... | collective-permute-start | bytes 1572872 | tf_op jit(solution)/shard_map/ppermute | solution.py:31
  46.5 8.3 %attend.2.a_ref = bf16[256,1024]{1,0:T(8,128)(2,1)S(1)} custom-call(s32[64]{0:T(128)S(1)} %copy-done.3, s32[192]{0:T(256)S(1)} %reshape.7.info_ref, s32[5]{0:T(128)S(1)} %copy-done, s32[192]{0:T(256)S(1)} %copy-done.2, bf16[7,256,128]{2,1,0:T(8,128)(2,1)S(1)} %bitcast.41, bf16[1024,128]{1,0:T(8,128)(2,1)S(1)} %constant_dynamic-update-slice_fusion.refs_0_, ...), custom_call_target="tpu_custom_call" | custom-call | flops 4000000000 | bytes 3000000 | tf_op jit(solution)/shard_map/attend/pallas_call | solution.py:185
  54.8 1.2 %collective-permute-done.13.b_ref = bf16[256,1024]{1,0:T(8,128)(2,1)S(1)} collective-permute-done((bf16[256,1024]{1,0:T(8,128)(2,1)S(1)}, bf16[256,1024]{1,0:T(8,128)(2,1)S(1)}, u32[]{:S(2)}, u32[]{:S(2)}) %collective-permute-start.13) | collective-permute-done | bytes 524320 | tf_op jit(solution)/shard_map/ppermute | solution.py:31
  56.0 4.8 %project.1 = (bf16[4,32,3584]{2,1,0:T(8,128)(2,1)S(1)}, bf16[4,32,3584]{2,1,0:T(8,128)(2,1)S(1)}) custom-call(s32[5]{0:T(128)S(1)} %copy-done, bf16[256,1024]{1,0:T(8,128)(2,1)S(1)} %attend.2.a_ref, bf16[256,1024]{1,0:T(8,128)(2,1)S(1)} %collective-permute-done.13.b_ref, bf16[896,3584]{1,0:T(8,128)(2,1)S(1)} %bitcast.39), custom_call_target="tpu_custom_call" | custom-call | flops 1640000000 | bytes 9000000 | tf_op jit(solution)/shard_map/project/pallas_call | solution.py:234
  60.8 3.5 %collective-permute-start.14 = (bf16[4,32,3584]{2,1,0:T(8,128)(2,1)S(1)}, bf16[4,32,3584]{2,1,0:T(8,128)(2,1)S(1)}, u32[]{:S(2)}, u32[]{:S(2)}) collective-permute-start(bf16[4,32,3584]{2,1,0:T(8,128)(2,1)S(1)} %get-tuple-element.8), channel_id=1, source_target_pairs={{1,0},{0,1},{3,2},{2,3},{5,4},{4,5},{7,6},{6,7},{9,8},{8,9},{11,10... | collective-permute-start | bytes 2752520 | tf_op jit(solution)/shard_map/ppermute | solution.py:31
  64.3 2.1 %collective-permute-done.14 = bf16[4,32,3584]{2,1,0:T(8,128)(2,1)S(1)} collective-permute-done((bf16[4,32,3584]{2,1,0:T(8,128)(2,1)S(1)}, bf16[4,32,3584]{2,1,0:T(8,128)(2,1)S(1)}, u32[]{:S(2)}, u32[]{:S(2)}) %collective-permute-start.14) | collective-permute-done | bytes 917536 | tf_op jit(solution)/shard_map/ppermute | solution.py:31
  66.7 3.1 %collective-permute-start.15 = (bf16[32,3584]{1,0:T(8,128)(2,1)S(1)}, bf16[32,3584]{1,0:T(8,128)(2,1)S(1)}, u32[]{:S(2)}, u32[]{:S(2)}) collective-permute-start(bf16[32,3584]{1,0:T(8,128)(2,1)S(1)} %get-tuple-element.11), channel_id=1, source_target_pairs={{6,0},{0,2},{2,4},{4,6},{7,1},{1,3},{3,5},{5,7},{14,8},{8,10},{10,... | collective-permute-start | bytes 688136 | tf_op jit(solution)/shard_map/ppermute | solution.py:31
  69.8 5.3 %collective-permute-start.17 = (bf16[32,3584]{1,0:T(8,128)(2,1)S(1)}, bf16[32,3584]{1,0:T(8,128)(2,1)S(1)}, u32[]{:S(2)}, u32[]{:S(2)}) collective-permute-start(bf16[32,3584]{1,0:T(8,128)(2,1)S(1)} %get-tuple-element.12), channel_id=1, source_target_pairs={{4,0},{6,2},{0,4},{2,6},{5,1},{7,3},{1,5},{3,7},{12,8},{14,10},{8,... | collective-permute-start | bytes 688136 | tf_op jit(solution)/shard_map/ppermute | solution.py:31
  75.1 2.4 %collective-permute-start.16 = (bf16[32,3584]{1,0:T(8,128)(2,1)S(1)}, bf16[32,3584]{1,0:T(8,128)(2,1)S(1)}, u32[]{:S(2)}, u32[]{:S(2)}) collective-permute-start(bf16[32,3584]{1,0:T(8,128)(2,1)S(1)} %get-tuple-element.13), channel_id=1, source_target_pairs={{2,0},{4,2},{6,4},{0,6},{3,1},{5,3},{7,5},{1,7},{10,8},{12,10},{14... | collective-permute-start | bytes 688136 | tf_op jit(solution)/shard_map/ppermute | solution.py:31
  77.5 1.4 %collective-permute-done.15 = bf16[32,3584]{1,0:T(8,128)(2,1)S(1)} collective-permute-done((bf16[32,3584]{1,0:T(8,128)(2,1)S(1)}, bf16[32,3584]{1,0:T(8,128)(2,1)S(1)}, u32[]{:S(2)}, u32[]{:S(2)}) %collective-permute-start.15) | collective-permute-done | bytes 229408 | tf_op jit(solution)/shard_map/ppermute | solution.py:31
  78.8 6.9 %collective-permute-done.17 = bf16[32,3584]{1,0:T(8,128)(2,1)S(1)} collective-permute-done((bf16[32,3584]{1,0:T(8,128)(2,1)S(1)}, bf16[32,3584]{1,0:T(8,128)(2,1)S(1)}, u32[]{:S(2)}, u32[]{:S(2)}) %collective-permute-start.17) | collective-permute-done | bytes 229408 | tf_op jit(solution)/shard_map/ppermute | solution.py:31
  85.8 11.4 %collective-permute-done.16 = bf16[32,3584]{1,0:T(8,128)(2,1)S(1)} collective-permute-done((bf16[32,3584]{1,0:T(8,128)(2,1)S(1)}, bf16[32,3584]{1,0:T(8,128)(2,1)S(1)}, u32[]{:S(2)}, u32[]{:S(2)}) %collective-permute-start.16) | collective-permute-done | bytes 229408 | tf_op jit(solution)/shard_map/ppermute | solution.py:31
  97.2 0.8 fusion.3
  (40 shorter events, 5.4 us)
Async XLA Ops:
  0.8 12.9 %collective-permute-start.2 = (bf16[256,128]{1,0:T(8,128)(2,1)S(1)}, bf16[256,128]{1,0:T(8,128)(2,1)S(1)}, u32[]{:S(2)}, u32[]{:S(2)}) collective-permute-start(bf16[256,128]{1,0:T(8,128)(2,1)S(1)} %pad_maximum_fusion), channel_id=1, source_target_pairs={{16,0},{24,8},{0,16},{8,24},{17,1},{25,9},{1,17},{9,25},{18,2},{26... | collective-permute-start | bytes 196616 | tf_op jit(solution)/shard_map/ppermute | solution.py:31
  4.7 7.4 %collective-permute-start.1 = (bf16[256,128]{1,0:T(8,128)(2,1)S(1)}, bf16[256,128]{1,0:T(8,128)(2,1)S(1)}, u32[]{:S(2)}, u32[]{:S(2)}) collective-permute-start(bf16[256,128]{1,0:T(8,128)(2,1)S(1)} %pad_maximum_fusion), channel_id=1, source_target_pairs={{8,0},{16,8},{24,16},{0,24},{9,1},{17,9},{25,17},{1,25},{10,2},{18... | collective-permute-start | bytes 196616 | tf_op jit(solution)/shard_map/ppermute | solution.py:31
  5.4 5.9 %collective-permute-start = (bf16[256,128]{1,0:T(8,128)(2,1)S(1)}, bf16[256,128]{1,0:T(8,128)(2,1)S(1)}, u32[]{:S(2)}, u32[]{:S(2)}) collective-permute-start(bf16[256,128]{1,0:T(8,128)(2,1)S(1)} %pad_maximum_fusion), channel_id=1, source_target_pairs={{24,0},{0,8},{8,16},{16,24},{25,1},{1,9},{9,17},{17,25},{26,2},{2,... | collective-permute-start | bytes 196616 | tf_op jit(solution)/shard_map/ppermute | solution.py:31
  6.1 11.2 %collective-permute-start.8 = (bf16[256,128]{1,0:T(8,128)(2,1)S(1)}, bf16[256,128]{1,0:T(8,128)(2,1)S(1)}, u32[]{:S(2)}, u32[]{:S(2)}) collective-permute-start(bf16[256,128]{1,0:T(8,128)(2,1)S(1)} %pad_maximum_fusion.1), channel_id=1, source_target_pairs={{128,0},{192,64},{0,128},{64,192},{129,1},{193,65},{1,129},{65,193... | collective-permute-start | bytes 196616 | tf_op jit(solution)/shard_map/ppermute | solution.py:31
  8.9 7.7 %collective-permute-start.7 = (bf16[256,128]{1,0:T(8,128)(2,1)S(1)}, bf16[256,128]{1,0:T(8,128)(2,1)S(1)}, u32[]{:S(2)}, u32[]{:S(2)}) collective-permute-start(bf16[256,128]{1,0:T(8,128)(2,1)S(1)} %pad_maximum_fusion.1), channel_id=1, source_target_pairs={{64,0},{128,64},{192,128},{0,192},{65,1},{129,65},{193,129},{1,193... | collective-permute-start | bytes 196616 | tf_op jit(solution)/shard_map/ppermute | solution.py:31
  11.3 4.4 %collective-permute-start.6 = (bf16[256,128]{1,0:T(8,128)(2,1)S(1)}, bf16[256,128]{1,0:T(8,128)(2,1)S(1)}, u32[]{:S(2)}, u32[]{:S(2)}) collective-permute-start(bf16[256,128]{1,0:T(8,128)(2,1)S(1)} %pad_maximum_fusion.1), channel_id=1, source_target_pairs={{192,0},{0,64},{64,128},{128,192},{193,1},{1,65},{65,129},{129,193... | collective-permute-start | bytes 196616 | tf_op jit(solution)/shard_map/ppermute | solution.py:31
  12.0 23.8 %collective-permute-start.12 = (bf16[7,256,128]{2,1,0:T(8,128)(2,1)}, bf16[7,256,128]{2,1,0:T(8,128)(2,1)S(1)}, u32[]{:S(2)}, u32[]{:S(2)}) collective-permute-start(bf16[7,256,128]{2,1,0:T(8,128)(2,1)} %bitcast.40), channel_id=1, source_target_pairs={{32,0},{0,32},{33,1},{1,33},{34,2},{2,34},{35,3},{3,35},{36,4},{4,... | collective-permute-start | bytes 1376264 | tf_op jit(solution)/shard_map/ppermute | solution.py:31
  13.8 7.0 %collective-permute-start.5 = (bf16[1024,128]{1,0:T(8,128)(2,1)S(1)}, bf16[1024,128]{1,0:T(8,128)(2,1)S(1)}, u32[]{:S(2)}, u32[]{:S(2)}) collective-permute-start(bf16[1024,128]{1,0:T(8,128)(2,1)S(1)} %constant_dynamic-update-slice_fusion.refs_0_), channel_id=1, source_target_pairs={{128,0},{192,64},{0,128},{64,192},{129,1},{193,65},{1,129},{65,193... | collective-permute-start | bytes 786440 | tf_op jit(solution)/shard_map/ppermute | solution.py:31
  15.7 10.2 %collective-permute-start.4 = (bf16[1024,128]{1,0:T(8,128)(2,1)S(1)}, bf16[1024,128]{1,0:T(8,128)(2,1)S(1)}, u32[]{:S(2)}, u32[]{:S(2)}) collective-permute-start(bf16[1024,128]{1,0:T(8,128)(2,1)S(1)} %constant_dynamic-update-slice_fusion.refs_0_), channel_id=1, source_target_pairs={{64,0},{128,64},{192,128},{0,192},{65,1},{129,65},{193,129},{1,193... | collective-permute-start | bytes 786440 | tf_op jit(solution)/shard_map/ppermute | solution.py:31
  16.6 14.2 %collective-permute-start.3 = (bf16[1024,128]{1,0:T(8,128)(2,1)S(1)}, bf16[1024,128]{1,0:T(8,128)(2,1)S(1)}, u32[]{:S(2)}, u32[]{:S(2)}) collective-permute-start(bf16[1024,128]{1,0:T(8,128)(2,1)S(1)} %constant_dynamic-update-slice_fusion.refs_0_), channel_id=1, source_target_pairs={{192,0},{0,64},{64,128},{128,192},{193,1},{1,65},{65,129},{129,193... | collective-permute-start | bytes 786440 | tf_op jit(solution)/shard_map/ppermute | solution.py:31
  17.3 13.5 %collective-permute-start.11 = (bf16[1024,128]{1,0:T(8,128)(2,1)S(1)}, bf16[1024,128]{1,0:T(8,128)(2,1)S(1)}, u32[]{:S(2)}, u32[]{:S(2)}) collective-permute-start(bf16[1024,128]{1,0:T(8,128)(2,1)S(1)} %constant_dynamic-update-slice_fusion.5.refs_4_), channel_id=1, source_target_pairs={{16,0},{24,8},{0,16},{8,24},{17,1},{25,9},{1,17},{9,25},{18,2},{26... | collective-permute-start | bytes 786440 | tf_op jit(solution)/shard_map/ppermute | solution.py:31
  20.8 10.1 %collective-permute-start.10 = (bf16[1024,128]{1,0:T(8,128)(2,1)S(1)}, bf16[1024,128]{1,0:T(8,128)(2,1)S(1)}, u32[]{:S(2)}, u32[]{:S(2)}) collective-permute-start(bf16[1024,128]{1,0:T(8,128)(2,1)S(1)} %constant_dynamic-update-slice_fusion.5.refs_4_), channel_id=1, source_target_pairs={{8,0},{16,8},{24,16},{0,24},{9,1},{17,9},{25,17},{1,25},{10,2},{18... | collective-permute-start | bytes 786440 | tf_op jit(solution)/shard_map/ppermute | solution.py:31
  25.9 9.9 %collective-permute-start.9 = (bf16[1024,128]{1,0:T(8,128)(2,1)S(1)}, bf16[1024,128]{1,0:T(8,128)(2,1)S(1)}, u32[]{:S(2)}, u32[]{:S(2)}) collective-permute-start(bf16[1024,128]{1,0:T(8,128)(2,1)S(1)} %constant_dynamic-update-slice_fusion.5.refs_4_), channel_id=1, source_target_pairs={{24,0},{0,8},{8,16},{16,24},{25,1},{1,9},{9,17},{17,25},{26,2},{2,... | collective-permute-start | bytes 786440 | tf_op jit(solution)/shard_map/ppermute | solution.py:31
  35.8 0.7 copy-start
  36.5 0.7 copy-start.1
  37.2 0.7 copy-start.3
  37.8 8.7 %copy-start.2 = (s32[192]{0:T(256)S(1)}, s32[192]{0:T(256)}, u32[]{:S(2)}) copy-start(s32[192]{0:T(256)} %table.1.table_ref) | copy-start | bytes 2308
  37.8 8.7 %copy-start.4 = (bf16[256,7,128]{2,0,1:T(8,128)(2,1)S(1)}, bf16[256,7,128]{2,0,1:T(8,128)(2,1)}, u32[]{:S(2)}) copy-start(bf16[256,7,128]{2,0,1:T(8,128)(2,1)} %param.6) | copy-start | bytes 1376260
  37.8 18.2 %slice-start = ((s8[6422528]{0:T(1024)(128)(4,1)}), s8[4194304]{0:T(1024)(128)(4,1)S(1)}, s32[]{:S(2)}) async-start(s8[6422528]{0:T(1024)(128)(4,1)} %bitcast.38), calls=%async_computation | async-start | bytes 8388608
  43.7 12.3 %slice-start.1 = ((s8[6422528]{0:T(1024)(128)(4,1)}), s8[2228224]{0:T(1024)(128)(4,1)S(1)}, s32[]{:S(2)}) async-start(s8[6422528]{0:T(1024)(128)(4,1)} %bitcast.38), calls=%async_computation.1 | async-start | bytes 4456448
  43.7 12.3 %collective-permute-start.13 = (bf16[256,1024]{1,0:T(8,128)(2,1)S(1)}, bf16[256,1024]{1,0:T(8,128)(2,1)S(1)}, u32[]{:S(2)}, u32[]{:S(2)}) collective-permute-start(bf16[256,1024]{1,0:T(8,128)(2,1)S(1)} %attend.3), channel_id=1, source_target_pairs={{32,0},{0,32},{33,1},{1,33},{34,2},{2,34},{35,3},{3,35},{36,4},{4,... | collective-permute-start | bytes 1572872 | tf_op jit(solution)/shard_map/ppermute | solution.py:31
  60.8 5.6 %collective-permute-start.14 = (bf16[4,32,3584]{2,1,0:T(8,128)(2,1)S(1)}, bf16[4,32,3584]{2,1,0:T(8,128)(2,1)S(1)}, u32[]{:S(2)}, u32[]{:S(2)}) collective-permute-start(bf16[4,32,3584]{2,1,0:T(8,128)(2,1)S(1)} %get-tuple-element.8), channel_id=1, source_target_pairs={{1,0},{0,1},{3,2},{2,3},{5,4},{4,5},{7,6},{6,7},{9,8},{8,9},{11,10... | collective-permute-start | bytes 2752520 | tf_op jit(solution)/shard_map/ppermute | solution.py:31
  66.7 12.1 %collective-permute-start.15 = (bf16[32,3584]{1,0:T(8,128)(2,1)S(1)}, bf16[32,3584]{1,0:T(8,128)(2,1)S(1)}, u32[]{:S(2)}, u32[]{:S(2)}) collective-permute-start(bf16[32,3584]{1,0:T(8,128)(2,1)S(1)} %get-tuple-element.11), channel_id=1, source_target_pairs={{6,0},{0,2},{2,4},{4,6},{7,1},{1,3},{3,5},{5,7},{14,8},{8,10},{10,... | collective-permute-start | bytes 688136 | tf_op jit(solution)/shard_map/ppermute | solution.py:31
  69.8 16.0 %collective-permute-start.17 = (bf16[32,3584]{1,0:T(8,128)(2,1)S(1)}, bf16[32,3584]{1,0:T(8,128)(2,1)S(1)}, u32[]{:S(2)}, u32[]{:S(2)}) collective-permute-start(bf16[32,3584]{1,0:T(8,128)(2,1)S(1)} %get-tuple-element.12), channel_id=1, source_target_pairs={{4,0},{6,2},{0,4},{2,6},{5,1},{7,3},{1,5},{3,7},{12,8},{14,10},{8,... | collective-permute-start | bytes 688136 | tf_op jit(solution)/shard_map/ppermute | solution.py:31
  75.1 22.1 %collective-permute-start.16 = (bf16[32,3584]{1,0:T(8,128)(2,1)S(1)}, bf16[32,3584]{1,0:T(8,128)(2,1)S(1)}, u32[]{:S(2)}, u32[]{:S(2)}) collective-permute-start(bf16[32,3584]{1,0:T(8,128)(2,1)S(1)} %get-tuple-element.13), channel_id=1, source_target_pairs={{2,0},{4,2},{6,4},{0,6},{3,1},{5,3},{7,5},{1,7},{10,8},{12,10},{14... | collective-permute-start | bytes 688136 | tf_op jit(solution)/shard_map/ppermute | solution.py:31
where the time goes:
time: 98.5 us; the launch traced here: 98 us
  starting transfers between devices  34.6 us (35%)
  waiting for transfers between devices  34.2 us (35%)
  Pallas kernels  21.9 us (22%)
  local copies, waits for them, and re-layouts  6.1 us (6%)
  other arithmetic  1.1 us (1%)
    ppermute x18, starting transfers between devices, shift(): lax.ppermute(value, axis, [((i + step) % size, i) for i in range(size)])  34.6 us
    ppermute x18, waiting for transfers between devices, shift(): lax.ppermute(value, axis, [((i + step) % size, i) for i in range(size)])  34.2 us
    pallas_call x2, Pallas kernels, attend(): pl.pallas_call(functools.partial(attend_kernel, flip), out_shape=jax.Shap...  14.2 us
    pallas_call x1, Pallas kernels, project(): pl.pallas_call(project_kernel, grid=(out_cols // tile,), out_shape=(piece...  4.78 us
    unnamed x21, local copies, waits for them, and re-layouts  4.4 us
    pallas_call x1, Pallas kernels, make_table(): pl.pallas_call(table_kernel, out_shape=jax.ShapeDtypeStruct((3 * BLOCKS,)...  2.92 us
  transfers between devices with their start and end apart: 18, of which 9 were waited for; matrix products, arithmetic and copies ran while one was open for 3% of the time, Pallas kernels for 11%

commit v1 on v0

v1 whole, which is shorter than its diff:
```python
import functools
import math

import jax
import jax.numpy as jnp
from jax import lax
from jax.experimental import pallas as pl
from jax.experimental.pallas import tpu as pltpu
from jax.sharding import Mesh, PartitionSpec as P

BLK = 128
HD = 128
GROUP = 7
ROWS = 256
FEATS = GROUP * HD
BLOCKS = 64
CHUNK = 16
LIST = 48
QUERY_AT = 3 * LIST
HEAD_AT = QUERY_AT + 16
TABLE = 256
MINUS = -1e30
SIZES = {"x": 4, "zl": 2, "y": 4, "zh": 4, "core": 2}
AXES = tuple(SIZES)
CTX = ("x", "zl", "y")
HEAD = ("zh", "core")
OFFSETS = (0, 1, -1, 2)
PLACES = (0, 4, 5, 1, 6, 2, 7, 3)
SMEM = pl.BlockSpec(memory_space=pltpu.SMEM)
VMEM = pl.BlockSpec(memory_space=pltpu.VMEM)
ANYWHERE = pl.BlockSpec(memory_space=pl.ANY)


def shift(value, axis, step):
    size = SIZES[axis]
    return lax.ppermute(value, axis, [((i + step) % size, i) for i in range(size)])


def table_kernel(order_ref, info_ref, table_ref, inv_ref):
    my_x, my_zl, my_y = (lax.axis_index(axis) for axis in CTX)

    def invert(block, _):
        inv_ref[order_ref[block]] = block
        return 0

    lax.fori_loop(0, BLOCKS, invert, 0)
    table_ref[HEAD_AT] = lax.axis_index("zh")
    table_ref[HEAD_AT + 1] = lax.axis_index("core")
    ends = []
    for i in range(4):
        pair_zl = my_zl ^ 1 if i < 2 else my_zl
        block = order_ref[((my_x * 2 + pair_zl) * 4 + my_y) * 2 + i % 2]
        last, kind = info_ref[1, block], info_ref[2, block]
        at = QUERY_AT + 4 * i
        table_ref[at], table_ref[at + 1], table_ref[at + 2] = block, kind, last
        ends.append(jnp.where(kind == 1, lax.div(last, BLK) - 1, block))

    def place(position, carry):
        count, seen = carry[0], carry[1:]
        block = inv_ref[position]
        ctx = block >> 1
        x_off, y_off = ((ctx >> 3) - my_x) & 3, ((ctx & 3) - my_y) & 3
        x_part, y_part = (x_off ^ (x_off >> 1)), (y_off ^ (y_off >> 1))
        here = ((ctx >> 2) & 1) == my_zl
        table_ref[count] = (x_part * 4 + y_part) * 2 + (block & 1)
        table_ref[LIST + count] = (y_part * 4 + x_part) * 2 + (block & 1)
        table_ref[2 * LIST + count] = position
        count = count + here.astype(jnp.int32)
        return (count,) + tuple(jnp.where(position == end, count, s) for end, s in zip(ends, seen))

    done = lax.fori_loop(0, BLOCKS, place, (jnp.int32(0),) * 5)
    for i in range(4):
        table_ref[QUERY_AT + 4 * i + 3] = done[1 + i]
    for i in range(BLOCKS // 2, LIST):
        table_ref[i] = 0
        table_ref[LIST + i] = 0
        table_ref[2 * LIST + i] = BLOCKS


def make_table(order, info):
    return pl.pallas_call(
        table_kernel,
        out_shape=jax.ShapeDtypeStruct((TABLE,), jnp.int32),
        in_specs=[SMEM, SMEM],
        out_specs=SMEM,
        scratch_shapes=[pltpu.SMEM((BLOCKS,), jnp.int32)],
        cost_estimate=pl.CostEstimate(flops=2_000_000_000, bytes_accessed=1000, transcendentals=0),
        name="table",
    )(order, info)


def attend_kernel(side, table_hbm, q_hbm, *refs):
    parts = refs[:8]
    out_hbm, table_ref, q_ref, out_ref, kv_ref, qs_ref, m_ref, l_ref, acc_ref, kv_sem, in_sem, out_sem = refs[8:]
    part_rows = parts[0].shape[0]
    half = 4 * part_rows
    table_copy = pltpu.make_async_copy(table_hbm, table_ref, in_sem.at[0])
    q_copy = pltpu.make_async_copy(q_hbm, q_ref, in_sem.at[1])
    copies = [
        pltpu.make_async_copy(part, kv_ref.at[pl.ds(i * part_rows, part_rows)], kv_sem.at[i])
        for i, part in zip(PLACES, parts)
    ]
    out_copies = [
        pltpu.make_async_copy(
            out_ref.at[pl.ds(t * BLK, BLK)], out_hbm.at[pl.ds(t * BLK, BLK)], out_sem.at[t]
        )
        for t in range(2)
    ]
    table_copy.start()
    q_copy.start()
    for copy in copies:
        copy.start()
    scale = math.log2(math.e) / math.sqrt(HD)
    rows = GROUP * BLK
    q_copy.wait()
    table_copy.wait()
    for copy in copies:
        copy.wait()

    def one_block(t, _):
        at = QUERY_AT + 4 * (2 * side + t)
        block, kind, last, count = table_ref[at], table_ref[at + 1], table_ref[at + 2], table_ref[at + 3]
        q_rows = pl.ds(pl.multiple_of(t * BLK, BLK), BLK)
        for h in range(GROUP):
            scaled = q_ref[h, q_rows, :].astype(jnp.float32) * scale
            high = scaled.astype(jnp.bfloat16)
            qs_ref[h * BLK : (h + 1) * BLK, 0:HD] = high
            qs_ref[h * BLK : (h + 1) * BLK, HD:] = (scaled - high.astype(jnp.float32)).astype(jnp.bfloat16)
        m_ref[...] = jnp.full_like(m_ref, MINUS)
        l_ref[...] = jnp.zeros_like(l_ref)
        acc_ref[...] = jnp.zeros_like(acc_ref)

        def step(begin, size, masked):
            key_list, value_list = [], []
            for j in range(size):
                key_at = pl.multiple_of(table_ref[begin + j] * BLK, BLK)
                value_at = pl.multiple_of(table_ref[LIST + begin + j] * BLK, BLK)
                key_list.append(kv_ref[pl.ds(key_at, BLK), :])
                value_list.append(kv_ref[pl.ds(value_at + half, BLK), :])
            key_tile = jnp.concatenate(key_list, axis=0)
            value_tile = jnp.concatenate(value_list, axis=0)
            twice = jnp.concatenate([key_tile, key_tile], axis=1)
            s = lax.dot_general(
                qs_ref[...], twice, (((1,), (1,)), ((), ())), preferred_element_type=jnp.float32
            )
            if masked:
                lane = lax.broadcasted_iota(jnp.int32, (rows, BLK), 1)
                row = lax.broadcasted_iota(jnp.int32, (rows, BLK), 0) & (BLK - 1)
                most = jnp.where(kind == 1, last - 1, block * BLK + row) - lane
                s = jnp.concatenate(
                    [
                        jnp.where(
                            table_ref[2 * LIST + begin + j] * BLK <= most, s[:, j * BLK : (j + 1) * BLK], MINUS
                        )
                        for j in range(size)
                    ],
                    axis=1,
                )
            m_old = m_ref[...]
            m_new = jnp.maximum(m_old, jnp.max(s, axis=1, keepdims=True))
            p = jnp.exp2(s - jnp.concatenate([m_new] * size, axis=1))
            fade = jnp.exp2(m_old - m_new)
            l_ref[...] = l_ref[...] * fade + sum(p[:, i * BLK : (i + 1) * BLK] for i in range(size))
            m_ref[...] = m_new
            acc_ref[...] = acc_ref[...] * fade + jnp.dot(
                p.astype(jnp.bfloat16), value_tile, preferred_element_type=jnp.float32
            )

        full = lax.div(jnp.maximum(count - 1, 0), CHUNK)

        def full_step(chunk, _):
            step(chunk * CHUNK, CHUNK, False)
            return 0

        lax.fori_loop(0, full, full_step, 0)
        rest = count - full * CHUNK
        for size in (4, 8, 12, 16):

            @pl.when((rest > size - 4) & (rest <= size))
            def _(size=size):
                step(full * CHUNK, size, True)

        lane = lax.broadcasted_iota(jnp.int32, (BLK, BLK), 1)
        stats = jnp.zeros((BLK, BLK), jnp.float32)
        for h in range(GROUP):
            part = slice(h * BLK, (h + 1) * BLK)
            total = jnp.sum(l_ref[part, :], axis=1, keepdims=True)
            safe = jnp.where(total > 0, total, 1.0)
            out_ref[q_rows, h * HD : (h + 1) * HD] = (acc_ref[part, :] / safe).astype(jnp.bfloat16)
            level = m_ref[part, :] + jnp.log2(safe)
            high = level.astype(jnp.bfloat16).astype(jnp.float32)
            middle = (level - high).astype(jnp.bfloat16).astype(jnp.float32)
            stats = jnp.where(lane == h, high, stats)
            stats = jnp.where(lane == 8 + h, middle, stats)
            stats = jnp.where(lane == 16 + h, level - high - middle, stats)
        out_ref[q_rows, FEATS:] = stats.astype(jnp.bfloat16)
        return 0

    def send_block(t, _):
        one_block(t, 0)
        for i in range(2):

            @pl.when(t == i)
            def _(i=i):
                out_copies[i].start()

        return 0

    lax.fori_loop(0, 2, send_block, 0)
    for copy in out_copies:
        copy.wait()


def attend(side, table, q, parts):
    part_rows = parts[0].shape[0]
    rows = GROUP * BLK
    return pl.pallas_call(
        functools.partial(attend_kernel, side),
        out_shape=jax.ShapeDtypeStruct((ROWS, FEATS + BLK), jnp.bfloat16),
        in_specs=[ANYWHERE] * 10,
        out_specs=ANYWHERE,
        scratch_shapes=[
            pltpu.SMEM((TABLE,), jnp.int32),
            pltpu.VMEM(q.shape, jnp.bfloat16),
            pltpu.VMEM((ROWS, FEATS + BLK), jnp.bfloat16),
            pltpu.VMEM((8 * part_rows, HD), jnp.bfloat16),
            pltpu.VMEM((rows, 2 * HD), jnp.bfloat16),
            pltpu.VMEM((rows, BLK), jnp.float32),
            pltpu.VMEM((rows, BLK), jnp.float32),
            pltpu.VMEM((rows, HD), jnp.float32),
            pltpu.SemaphoreType.DMA((8,)),
            pltpu.SemaphoreType.DMA((2,)),
            pltpu.SemaphoreType.DMA((2,)),
        ],
        compiler_params=pltpu.CompilerParams(vmem_limit_bytes=40 * 1024 * 1024),
        cost_estimate=pl.CostEstimate(flops=4_000_000_000, bytes_accessed=3_000_000, transcendentals=4_000_000),
        name="attend",
    )(table, q, *parts)


def project_kernel(table_ref, a_ref, b_ref, w_ref, keep_ref, send_ref, att_ref):
    my_zh, my_core = table_ref[HEAD_AT], table_ref[HEAD_AT + 1]

    @pl.when(pl.program_id(0) == 0)
    def _():
        stats_a = a_ref[:, FEATS:].astype(jnp.float32)
        stats_b = b_ref[:, FEATS:].astype(jnp.float32)
        for h in range(GROUP):

            def level(stats):
                return stats[:, h : h + 1] + stats[:, 8 + h : 9 + h] + stats[:, 16 + h : 17 + h]

            weight_a = 1.0 / (1.0 + jnp.exp2(level(stats_b) - level(stats_a)))
            cols = slice(h * HD, (h + 1) * HD)
            a, b = a_ref[:, cols].astype(jnp.float32), b_ref[:, cols].astype(jnp.float32)
            att_ref[:, cols] = (b + (a - b) * weight_a).astype(jnp.bfloat16)

    tile = keep_ref.shape[2]
    cols = pl.ds(pl.multiple_of(pl.program_id(0) * tile, tile), tile)
    res = jnp.dot(att_ref[...], w_ref[:, cols], preferred_element_type=jnp.float32).astype(jnp.bfloat16)
    for z in range(4):
        to = (z - my_zh) & 3
        zero, one = res[z * 64 : z * 64 + 32, :], res[z * 64 + 32 : z * 64 + 64, :]
        keep_ref[to] = jnp.where(my_core == 0, zero, one)
        send_ref[to] = jnp.where(my_core == 0, one, zero)


def project(table, a, b, w):
    out_cols = w.shape[1]
    tile = 512
    piece = jax.ShapeDtypeStruct((4, 32, out_cols), jnp.bfloat16)
    out_spec = pl.BlockSpec((4, 32, tile), lambda i: (0, 0, i))
    return pl.pallas_call(
        project_kernel,
        grid=(out_cols // tile,),
        out_shape=(piece, piece),
        in_specs=[
            SMEM,
            pl.BlockSpec(a.shape, lambda i: (0, 0)),
            pl.BlockSpec(b.shape, lambda i: (0, 0)),
            pl.BlockSpec(w.shape, lambda i: (0, 0)),
        ],
        out_specs=(out_spec, out_spec),
        scratch_shapes=[pltpu.VMEM((ROWS, FEATS), jnp.bfloat16)],
        compiler_params=pltpu.CompilerParams(vmem_limit_bytes=24 * 1024 * 1024),
        cost_estimate=pl.CostEstimate(flops=1_640_000_000, bytes_accessed=9_000_000, transcendentals=1792),
        name="project",
    )(table, a, b, w)


def body(queries, keys, values, out_weight, segment_info, block_order):
    k, v = keys[:, 0, :], values[:, 0, :]
    q = jnp.transpose(queries, (1, 0, 2))
    other_q = shift(q, "zl", 1)
    k = [k] + [shift(k, "y", o) for o in OFFSETS[1:]]
    v = [v] + [shift(v, "x", o) for o in OFFSETS[1:]]
    table = make_table(block_order, segment_info.T)
    k, v, table, other_q = lax.optimization_barrier((k, v, table, other_q))
    k = jnp.concatenate(k, axis=0)
    v = jnp.concatenate(v, axis=0)
    k, v = lax.optimization_barrier((k, v))
    parts = [k, v]
    for o in OFFSETS[1:]:
        parts += [shift(v, "y", o), shift(k, "x", o)]
    other = attend(0, table, other_q, parts)
    back = shift(other, "zl", 1)
    own = attend(1, table, q, parts)
    keep, send = project(table, own, back, out_weight)
    pieces = keep.astype(jnp.float32) + shift(send, "core", 1).astype(jnp.float32)
    low = pieces.astype(jnp.bfloat16)
    top, bottom = slice(0, 16), slice(16, 32)
    ahead = jnp.concatenate([low[2, top], low[1, bottom]], axis=0)
    back = jnp.concatenate([low[2, bottom], low[3, top]], axis=0)
    from_behind, from_ahead = shift(ahead, "zh", -1), shift(back, "zh", 1)
    ahead = (pieces[1, top] + from_behind[top].astype(jnp.float32)).astype(jnp.bfloat16)
    back = (pieces[3, bottom] + from_ahead[top].astype(jnp.float32)).astype(jnp.bfloat16)
    last_behind, last_ahead = shift(ahead, "zh", -1), shift(back, "zh", 1)
    behind = jnp.concatenate([last_behind, from_behind[bottom]], axis=0)
    beyond = jnp.concatenate([from_ahead[bottom], last_ahead], axis=0)
    total = pieces[0] + behind.astype(jnp.float32) + beyond.astype(jnp.float32)
    return total.astype(jnp.bfloat16)


def solution(mesh):
    fine = Mesh(mesh.devices.reshape(tuple(SIZES.values())), AXES)
    placed = (
        P(CTX, HEAD, None),
        P(CTX, HEAD, None),
        P(CTX, HEAD, None),
        P(HEAD, None),
        P(),
        P(),
    )
    return jax.shard_map(body, mesh=fine, in_specs=placed, out_specs=P(AXES, None), check_vma=False)
```

time: 98.5 us -> 93.8 us (0.952)
  the two profiles are of different devices: /device:TPU:1 before, /device:TPU:16 now
where the time goes in v1:
time: 93.8 us; the launch traced here: 95.5 us
  starting transfers between devices  37.9 us (40%)
  waiting for transfers between devices  29.6 us (32%)
  Pallas kernels  25.9 us (28%)
  other arithmetic  1.18 us (1%)
    ppermute x19, starting transfers between devices, shift(): lax.ppermute(value, axis, [((i + step) % size, i) for i in range(size)])  37.9 us
    ppermute x19, waiting for transfers between devices, shift(): lax.ppermute(value, axis, [((i + step) % size, i) for i in range(size)])  29.6 us
    pallas_call x2, Pallas kernels, attend(): pl.pallas_call(functools.partial(attend_kernel, side), out_shape=jax.Shap...  18.4 us
    pallas_call x1, Pallas kernels, project(): pl.pallas_call(project_kernel, grid=(out_cols // tile,), out_shape=(piece...  4.46 us
    pallas_call x1, Pallas kernels, make_table(): pl.pallas_call(table_kernel, out_shape=jax.ShapeDtypeStruct((TABLE,), jnp...  3.05 us
  transfers between devices with their start and end apart: 19, of which 10 were waited for; matrix products, arithmetic and copies ran while one was open for 0% of the time, Pallas kernels for 16%

profile of v1, /device:TPU:16, one launch (start us, length us, event | category | flops | bytes accessed | tf_op | source)
XLA Modules:
  0.0 95.5 jit_solution(3246069875541128383)
XLA Ops:
  0.0 1.9 %collective-permute-start.6 = (bf16[7,256,128]{2,1,0:T(8,128)(2,1)}, bf16[7,256,128]{2,1,0:T(8,128)(2,1)S(1)}, u32[]{:S(2)}, u32[]{:S(2)}) collective-permute-start(bf16[7,256,128]{2,1,0:T(8,128)(2,1)} %bitcast.34), channel_id=1, source_target_pairs={{32,0},{0,32},{33,1},{1,33},{34,2},{2,34},{35,3},{3,35},{36,4},{4,... | collective-permute-start | bytes 1376264 | tf_op jit(solution)/shard_map/ppermute | solution.py:36
  1.9 0.3 collective-permute-start.2
  2.3 2.2 %collective-permute-start.1 = (bf16[256,128]{1,0:T(8,128)(2,1)}, bf16[256,128]{1,0:T(8,128)(2,1)S(1)}, u32[]{:S(2)}, u32[]{:S(2)}) collective-permute-start(bf16[256,128]{1,0:T(8,128)(2,1)} %bitcast.37), channel_id=1, source_target_pairs={{24,0},{0,8},{8,16},{16,24},{25,1},{1,9},{9,17},{17,25},{26,2},{2,... | collective-permute-start | bytes 196616 | tf_op jit(solution)/shard_map/ppermute | solution.py:36
  4.7 3.0 %collective-permute-start.5 = (bf16[256,128]{1,0:T(8,128)(2,1)}, bf16[256,128]{1,0:T(8,128)(2,1)S(1)}, u32[]{:S(2)}, u32[]{:S(2)}) collective-permute-start(bf16[256,128]{1,0:T(8,128)(2,1)} %bitcast.40), channel_id=1, source_target_pairs={{128,0},{192,64},{0,128},{64,192},{129,1},{193,65},{1,129},{65,193... | collective-permute-start | bytes 196616 | tf_op jit(solution)/shard_map/ppermute | solution.py:36
  7.9 1.5 %collective-permute-start.4 = (bf16[256,128]{1,0:T(8,128)(2,1)}, bf16[256,128]{1,0:T(8,128)(2,1)S(1)}, u32[]{:S(2)}, u32[]{:S(2)}) collective-permute-start(bf16[256,128]{1,0:T(8,128)(2,1)} %bitcast.41), channel_id=1, source_target_pairs={{192,0},{0,64},{64,128},{128,192},{193,1},{1,65},{65,129},{129,193... | collective-permute-start | bytes 196616 | tf_op jit(solution)/shard_map/ppermute | solution.py:36
  9.4 1.7 %collective-permute-start.3 = (bf16[256,128]{1,0:T(8,128)(2,1)}, bf16[256,128]{1,0:T(8,128)(2,1)S(1)}, u32[]{:S(2)}, u32[]{:S(2)}) collective-permute-start(bf16[256,128]{1,0:T(8,128)(2,1)} %bitcast.42), channel_id=1, source_target_pairs={{64,0},{128,64},{192,128},{0,192},{65,1},{129,65},{193,129},{1,193... | collective-permute-start | bytes 196616 | tf_op jit(solution)/shard_map/ppermute | solution.py:36
  11.1 3.1 %table.1.table_hbm.table_ref = s32[256]{0:T(256)} custom-call(s32[64]{0:T(128)} %order_ref.1, s32[3,64]{1,0:T(4,128)} %bitcast.44), custom_call_target="tpu_custom_call" | custom-call | flops 2000000000 | bytes 1000 | tf_op jit(solution)/shard_map/table/pallas_call | solution.py:81
  14.3 2.4 %collective-permute-start.12 = (bf16[1024,128]{1,0:T(8,128)(2,1)S(1)}, bf16[1024,128]{1,0:T(8,128)(2,1)S(1)}, u32[]{:S(2)}, u32[]{:S(2)}) collective-permute-start(bf16[1024,128]{1,0:T(8,128)(2,1)S(1)} %get-tuple-element.28.refs_0_), channel_id=1, source_target_pairs={{128,0},{192,64},{0,128},{64,192},{129,1},{193,65},{1,129},{65,193... | collective-permute-start | bytes 786440 | tf_op jit(solution)/shard_map/ppermute | solution.py:36
  16.8 1.1 %collective-permute-start.10 = (bf16[1024,128]{1,0:T(8,128)(2,1)S(1)}, bf16[1024,128]{1,0:T(8,128)(2,1)S(1)}, u32[]{:S(2)}, u32[]{:S(2)}) collective-permute-start(bf16[1024,128]{1,0:T(8,128)(2,1)S(1)} %get-tuple-element.28.refs_0_), channel_id=1, source_target_pairs={{192,0},{0,64},{64,128},{128,192},{193,1},{1,65},{65,129},{129,193... | collective-permute-start | bytes 786440 | tf_op jit(solution)/shard_map/ppermute | solution.py:36
  17.8 2.2 %collective-permute-start.8 = (bf16[1024,128]{1,0:T(8,128)(2,1)S(1)}, bf16[1024,128]{1,0:T(8,128)(2,1)S(1)}, u32[]{:S(2)}, u32[]{:S(2)}) collective-permute-start(bf16[1024,128]{1,0:T(8,128)(2,1)S(1)} %get-tuple-element.28.refs_0_), channel_id=1, source_target_pairs={{64,0},{128,64},{192,128},{0,192},{65,1},{129,65},{193,129},{1,193... | collective-permute-start | bytes 786440 | tf_op jit(solution)/shard_map/ppermute | solution.py:36
  20.0 2.3 %collective-permute-start.11 = (bf16[1024,128]{1,0:T(8,128)(2,1)S(1)}, bf16[1024,128]{1,0:T(8,128)(2,1)S(1)}, u32[]{:S(2)}, u32[]{:S(2)}) collective-permute-start(bf16[1024,128]{1,0:T(8,128)(2,1)S(1)} %get-tuple-element.29.refs_1_), channel_id=1, source_target_pairs={{16,0},{24,8},{0,16},{8,24},{17,1},{25,9},{1,17},{9,25},{18,2},{26... | collective-permute-start | bytes 786440 | tf_op jit(solution)/shard_map/ppermute | solution.py:36
  22.3 0.5 collective-permute-start.9
  22.8 2.2 %collective-permute-done.12.refs_7_ = bf16[1024,128]{1,0:T(8,128)(2,1)S(1)} collective-permute-done((bf16[1024,128]{1,0:T(8,128)(2,1)S(1)}, bf16[1024,128]{1,0:T(8,128)(2,1)S(1)}, u32[]{:S(2)}, u32[]{:S(2)}) %collective-permute-start.12) | collective-permute-done | bytes 262176 | tf_op jit(solution)/shard_map/ppermute | solution.py:36
  24.9 1.8 %collective-permute-start.7 = (bf16[1024,128]{1,0:T(8,128)(2,1)S(1)}, bf16[1024,128]{1,0:T(8,128)(2,1)S(1)}, u32[]{:S(2)}, u32[]{:S(2)}) collective-permute-start(bf16[1024,128]{1,0:T(8,128)(2,1)S(1)} %get-tuple-element.29.refs_1_), channel_id=1, source_target_pairs={{8,0},{16,8},{24,16},{0,24},{9,1},{17,9},{25,17},{1,25},{10,2},{18... | collective-permute-start | bytes 786440 | tf_op jit(solution)/shard_map/ppermute | solution.py:36
  26.7 1.0 %collective-permute-done.10.refs_5_ = bf16[1024,128]{1,0:T(8,128)(2,1)S(1)} collective-permute-done((bf16[1024,128]{1,0:T(8,128)(2,1)S(1)}, bf16[1024,128]{1,0:T(8,128)(2,1)S(1)}, u32[]{:S(2)}, u32[]{:S(2)}) %collective-permute-start.10) | collective-permute-done | bytes 262176 | tf_op jit(solution)/shard_map/ppermute | solution.py:36
  27.7 2.3 %collective-permute-done.11.refs_6_ = bf16[1024,128]{1,0:T(8,128)(2,1)S(1)} collective-permute-done((bf16[1024,128]{1,0:T(8,128)(2,1)S(1)}, bf16[1024,128]{1,0:T(8,128)(2,1)S(1)}, u32[]{:S(2)}, u32[]{:S(2)}) %collective-permute-start.11) | collective-permute-done | bytes 262176 | tf_op jit(solution)/shard_map/ppermute | solution.py:36
  30.0 2.7 %collective-permute-done.9.refs_4_ = bf16[1024,128]{1,0:T(8,128)(2,1)S(1)} collective-permute-done((bf16[1024,128]{1,0:T(8,128)(2,1)S(1)}, bf16[1024,128]{1,0:T(8,128)(2,1)S(1)}, u32[]{:S(2)}, u32[]{:S(2)}) %collective-permute-start.9) | collective-permute-done | bytes 262176 | tf_op jit(solution)/shard_map/ppermute | solution.py:36
  32.7 0.7 copy-done
  33.4 6.6 %attend.3 = bf16[256,1024]{1,0:T(8,128)(2,1)S(1)} custom-call(s32[256]{0:T(256)S(1)} %copy-done, bf16[7,256,128]{2,1,0:T(8,128)(2,1)S(1)} %collective-permute-done.6.q_hbm, bf16[1024,128]{1,0:T(8,128)(2,1)S(1)} %get-tuple-element.28.refs_0_, bf16[1024,128]{1,0:T(8,128)(2,1)S(1)} %get-tuple-element.29.refs_1_, ...), custom_call_target="tpu_custom_call" | custom-call | flops 4000000000 | bytes 3000000 | tf_op jit(solution)/shard_map/attend/pallas_call | solution.py:217
  40.0 6.3 %collective-permute-start.13 = (bf16[256,1024]{1,0:T(8,128)(2,1)S(1)}, bf16[256,1024]{1,0:T(8,128)(2,1)S(1)}, u32[]{:S(2)}, u32[]{:S(2)}) collective-permute-start(bf16[256,1024]{1,0:T(8,128)(2,1)S(1)} %attend.3), channel_id=1, source_target_pairs={{32,0},{0,32},{33,1},{1,33},{34,2},{2,34},{35,3},{3,35},{36,4},{4,... | collective-permute-start | bytes 1572872 | tf_op jit(solution)/shard_map/ppermute | solution.py:36
  46.3 11.8 %attend.2.a_ref = bf16[256,1024]{1,0:T(8,128)(2,1)S(1)} custom-call(s32[256]{0:T(256)S(1)} %copy-done, bf16[7,256,128]{2,1,0:T(8,128)(2,1)S(1)} %bitcast.35, bf16[1024,128]{1,0:T(8,128)(2,1)S(1)} %get-tuple-element.28.refs_0_, bf16[1024,128]{1,0:T(8,128)(2,1)S(1)} %get-tuple-element.29.refs_1_, bf16[1024,128]{1,0:T(8,128)(2,1)S(1)} %collective-permute-done.7.refs_2_, ...), custom_call_target="tpu_custom_call" | custom-call | flops 4000000000 | bytes 3000000 | tf_op jit(solution)/shard_map/attend/pallas_call | solution.py:217
  58.1 4.5 %project.1 = (bf16[4,32,3584]{2,1,0:T(8,128)(2,1)S(1)}, bf16[4,32,3584]{2,1,0:T(8,128)(2,1)S(1)}) custom-call(s32[256]{0:T(256)S(1)} %copy-done, bf16[256,1024]{1,0:T(8,128)(2,1)S(1)} %attend.2.a_ref, bf16[256,1024]{1,0:T(8,128)(2,1)S(1)} %collective-permute-done.13.b_ref, bf16[896,3584]{1,0:T(8,128)(2,1)S(1)} %bitcast.33), custom_call_target="tpu_custom_call" | custom-call | flops 1640000000 | bytes 9000000 | tf_op jit(solution)/shard_map/project/pallas_call | solution.py:273
  62.6 2.5 %collective-permute-done.14 = bf16[4,32,3584]{2,1,0:T(8,128)(2,1)S(1)} collective-permute-done((bf16[4,32,3584]{2,1,0:T(8,128)(2,1)S(1)}, bf16[4,32,3584]{2,1,0:T(8,128)(2,1)S(1)}, u32[]{:S(2)}, u32[]{:S(2)}) %collective-permute-start.14) | collective-permute-done | bytes 917536 | tf_op jit(solution)/shard_map/ppermute | solution.py:36
  65.5 3.6 %collective-permute-start.15 = (bf16[32,3584]{1,0:T(8,128)(2,1)S(1)}, bf16[32,3584]{1,0:T(8,128)(2,1)S(1)}, u32[]{:S(2)}, u32[]{:S(2)}) collective-permute-start(bf16[32,3584]{1,0:T(8,128)(2,1)S(1)} %pad_maximum_fusion.2), channel_id=1, source_target_pairs={{6,0},{0,2},{2,4},{4,6},{7,1},{1,3},{3,5},{5,7},{14,8},{8,10},{10,... | collective-permute-start | bytes 688136 | tf_op jit(solution)/shard_map/ppermute | solution.py:36
  69.1 2.8 %collective-permute-start.17 = (bf16[32,3584]{1,0:T(8,128)(2,1)S(1)}, bf16[32,3584]{1,0:T(8,128)(2,1)S(1)}, u32[]{:S(2)}, u32[]{:S(2)}) collective-permute-start(bf16[32,3584]{1,0:T(8,128)(2,1)S(1)} %pad_maximum_fusion.3), channel_id=1, source_target_pairs={{2,0},{4,2},{6,4},{0,6},{3,1},{5,3},{7,5},{1,7},{10,8},{12,10},{14... | collective-permute-start | bytes 688136 | tf_op jit(solution)/shard_map/ppermute | solution.py:36
  71.9 7.0 %collective-permute-done.15 = bf16[32,3584]{1,0:T(8,128)(2,1)S(1)} collective-permute-done((bf16[32,3584]{1,0:T(8,128)(2,1)S(1)}, bf16[32,3584]{1,0:T(8,128)(2,1)S(1)}, u32[]{:S(2)}, u32[]{:S(2)}) %collective-permute-start.15) | collective-permute-done | bytes 229408 | tf_op jit(solution)/shard_map/ppermute | solution.py:36
  78.9 4.9 %collective-permute-done.17 = bf16[32,3584]{1,0:T(8,128)(2,1)S(1)} collective-permute-done((bf16[32,3584]{1,0:T(8,128)(2,1)S(1)}, bf16[32,3584]{1,0:T(8,128)(2,1)S(1)}, u32[]{:S(2)}, u32[]{:S(2)}) %collective-permute-start.17) | collective-permute-done | bytes 229408 | tf_op jit(solution)/shard_map/ppermute | solution.py:36
  83.9 2.8 %collective-permute-start.18 = (bf16[16,3584]{1,0:T(8,128)(2,1)S(1)}, bf16[16,3584]{1,0:T(8,128)(2,1)S(1)}, u32[]{:S(2)}, u32[]{:S(2)}) collective-permute-start(bf16[16,3584]{1,0:T(8,128)(2,1)S(1)} %get-tuple-element.33), channel_id=1, source_target_pairs={{2,0},{4,2},{6,4},{0,6},{3,1},{5,3},{7,5},{1,7},{10,8},{12,10},{14... | collective-permute-start | bytes 344072 | tf_op jit(solution)/shard_map/ppermute | solution.py:36
  86.7 1.2 %collective-permute-start.16 = (bf16[16,3584]{1,0:T(8,128)(2,1)S(1)}, bf16[16,3584]{1,0:T(8,128)(2,1)S(1)}, u32[]{:S(2)}, u32[]{:S(2)}) collective-permute-start(bf16[16,3584]{1,0:T(8,128)(2,1)S(1)} %get-tuple-element.34), channel_id=1, source_target_pairs={{6,0},{0,2},{2,4},{4,6},{7,1},{1,3},{3,5},{5,7},{14,8},{8,10},{10,... | collective-permute-start | bytes 344072 | tf_op jit(solution)/shard_map/ppermute | solution.py:36
  87.9 4.1 %collective-permute-done.18 = bf16[16,3584]{1,0:T(8,128)(2,1)S(1)} collective-permute-done((bf16[16,3584]{1,0:T(8,128)(2,1)S(1)}, bf16[16,3584]{1,0:T(8,128)(2,1)S(1)}, u32[]{:S(2)}, u32[]{:S(2)}) %collective-permute-start.18) | collective-permute-done | bytes 114720 | tf_op jit(solution)/shard_map/ppermute | solution.py:36
  92.0 2.7 %collective-permute-done.16 = bf16[16,3584]{1,0:T(8,128)(2,1)S(1)} collective-permute-done((bf16[16,3584]{1,0:T(8,128)(2,1)S(1)}, bf16[16,3584]{1,0:T(8,128)(2,1)S(1)}, u32[]{:S(2)}, u32[]{:S(2)}) %collective-permute-start.16) | collective-permute-done | bytes 114720 | tf_op jit(solution)/shard_map/ppermute | solution.py:36
  94.7 0.8 fusion.2
  (32 shorter events, 1.0 us)
Async XLA Ops:
  0.0 14.2 %collective-permute-start.6 = (bf16[7,256,128]{2,1,0:T(8,128)(2,1)}, bf16[7,256,128]{2,1,0:T(8,128)(2,1)S(1)}, u32[]{:S(2)}, u32[]{:S(2)}) collective-permute-start(bf16[7,256,128]{2,1,0:T(8,128)(2,1)} %bitcast.34), channel_id=1, source_target_pairs={{32,0},{0,32},{33,1},{1,33},{34,2},{2,34},{35,3},{3,35},{36,4},{4,... | collective-permute-start | bytes 1376264 | tf_op jit(solution)/shard_map/ppermute | solution.py:36
  1.9 6.0 %collective-permute-start.2 = (bf16[256,128]{1,0:T(8,128)(2,1)}, bf16[256,128]{1,0:T(8,128)(2,1)S(1)}, u32[]{:S(2)}, u32[]{:S(2)}) collective-permute-start(bf16[256,128]{1,0:T(8,128)(2,1)} %bitcast.36), channel_id=1, source_target_pairs={{16,0},{24,8},{0,16},{8,24},{17,1},{25,9},{1,17},{9,25},{18,2},{26... | collective-permute-start | bytes 196616 | tf_op jit(solution)/shard_map/ppermute | solution.py:36
  2.3 7.1 %collective-permute-start.1 = (bf16[256,128]{1,0:T(8,128)(2,1)}, bf16[256,128]{1,0:T(8,128)(2,1)S(1)}, u32[]{:S(2)}, u32[]{:S(2)}) collective-permute-start(bf16[256,128]{1,0:T(8,128)(2,1)} %bitcast.37), channel_id=1, source_target_pairs={{24,0},{0,8},{8,16},{16,24},{25,1},{1,9},{9,17},{17,25},{26,2},{2,... | collective-permute-start | bytes 196616 | tf_op jit(solution)/shard_map/ppermute | solution.py:36
  4.4 9.8 %collective-permute-start = (bf16[256,128]{1,0:T(8,128)(2,1)}, bf16[256,128]{1,0:T(8,128)(2,1)S(1)}, u32[]{:S(2)}, u32[]{:S(2)}) collective-permute-start(bf16[256,128]{1,0:T(8,128)(2,1)} %bitcast.38), channel_id=1, source_target_pairs={{8,0},{16,8},{24,16},{0,24},{9,1},{17,9},{25,17},{1,25},{10,2},{18... | collective-permute-start | bytes 196616 | tf_op jit(solution)/shard_map/ppermute | solution.py:36
  4.7 9.5 %collective-permute-start.5 = (bf16[256,128]{1,0:T(8,128)(2,1)}, bf16[256,128]{1,0:T(8,128)(2,1)S(1)}, u32[]{:S(2)}, u32[]{:S(2)}) collective-permute-start(bf16[256,128]{1,0:T(8,128)(2,1)} %bitcast.40), channel_id=1, source_target_pairs={{128,0},{192,64},{0,128},{64,192},{129,1},{193,65},{1,129},{65,193... | collective-permute-start | bytes 196616 | tf_op jit(solution)/shard_map/ppermute | solution.py:36
  7.9 6.3 %collective-permute-start.4 = (bf16[256,128]{1,0:T(8,128)(2,1)}, bf16[256,128]{1,0:T(8,128)(2,1)S(1)}, u32[]{:S(2)}, u32[]{:S(2)}) collective-permute-start(bf16[256,128]{1,0:T(8,128)(2,1)} %bitcast.41), channel_id=1, source_target_pairs={{192,0},{0,64},{64,128},{128,192},{193,1},{1,65},{65,129},{129,193... | collective-permute-start | bytes 196616 | tf_op jit(solution)/shard_map/ppermute | solution.py:36
  9.4 4.8 %collective-permute-start.3 = (bf16[256,128]{1,0:T(8,128)(2,1)}, bf16[256,128]{1,0:T(8,128)(2,1)S(1)}, u32[]{:S(2)}, u32[]{:S(2)}) collective-permute-start(bf16[256,128]{1,0:T(8,128)(2,1)} %bitcast.42), channel_id=1, source_target_pairs={{64,0},{128,64},{192,128},{0,192},{65,1},{129,65},{193,129},{1,193... | collective-permute-start | bytes 196616 | tf_op jit(solution)/shard_map/ppermute | solution.py:36
  11.1 3.1 %copy-start.2 = (bf16[256,1,128]{2,0,1:T(8,128)(2,1)S(1)}, bf16[256,1,128]{2,0,1:T(8,128)(2,1)}, u32[]{:S(2)}) copy-start(bf16[256,1,128]{2,0,1:T(8,128)(2,1)} %param.7) | copy-start | bytes 196612
  11.1 3.1 %copy-start.3 = (bf16[256,1,128]{2,0,1:T(8,128)(2,1)S(1)}, bf16[256,1,128]{2,0,1:T(8,128)(2,1)}, u32[]{:S(2)}) copy-start(bf16[256,1,128]{2,0,1:T(8,128)(2,1)} %param.8) | copy-start | bytes 196612
  14.3 32.0 %copy-start.1 = (bf16[256,7,128]{2,0,1:T(8,128)(2,1)S(1)}, bf16[256,7,128]{2,0,1:T(8,128)(2,1)}, u32[]{:S(2)}) copy-start(bf16[256,7,128]{2,0,1:T(8,128)(2,1)} %param.6) | copy-start | bytes 1376260
  14.3 10.6 %collective-permute-start.12 = (bf16[1024,128]{1,0:T(8,128)(2,1)S(1)}, bf16[1024,128]{1,0:T(8,128)(2,1)S(1)}, u32[]{:S(2)}, u32[]{:S(2)}) collective-permute-start(bf16[1024,128]{1,0:T(8,128)(2,1)S(1)} %get-tuple-element.28.refs_0_), channel_id=1, source_target_pairs={{128,0},{192,64},{0,128},{64,192},{129,1},{193,65},{1,129},{65,193... | collective-permute-start | bytes 786440 | tf_op jit(solution)/shard_map/ppermute | solution.py:36
  16.8 10.9 %collective-permute-start.10 = (bf16[1024,128]{1,0:T(8,128)(2,1)S(1)}, bf16[1024,128]{1,0:T(8,128)(2,1)S(1)}, u32[]{:S(2)}, u32[]{:S(2)}) collective-permute-start(bf16[1024,128]{1,0:T(8,128)(2,1)S(1)} %get-tuple-element.28.refs_0_), channel_id=1, source_target_pairs={{192,0},{0,64},{64,128},{128,192},{193,1},{1,65},{65,129},{129,193... | collective-permute-start | bytes 786440 | tf_op jit(solution)/shard_map/ppermute | solution.py:36
  17.8 9.9 %collective-permute-start.8 = (bf16[1024,128]{1,0:T(8,128)(2,1)S(1)}, bf16[1024,128]{1,0:T(8,128)(2,1)S(1)}, u32[]{:S(2)}, u32[]{:S(2)}) collective-permute-start(bf16[1024,128]{1,0:T(8,128)(2,1)S(1)} %get-tuple-element.28.refs_0_), channel_id=1, source_target_pairs={{64,0},{128,64},{192,128},{0,192},{65,1},{129,65},{193,129},{1,193... | collective-permute-start | bytes 786440 | tf_op jit(solution)/shard_map/ppermute | solution.py:36
  20.0 10.0 %collective-permute-start.11 = (bf16[1024,128]{1,0:T(8,128)(2,1)S(1)}, bf16[1024,128]{1,0:T(8,128)(2,1)S(1)}, u32[]{:S(2)}, u32[]{:S(2)}) collective-permute-start(bf16[1024,128]{1,0:T(8,128)(2,1)S(1)} %get-tuple-element.29.refs_1_), channel_id=1, source_target_pairs={{16,0},{24,8},{0,16},{8,24},{17,1},{25,9},{1,17},{9,25},{18,2},{26... | collective-permute-start | bytes 786440 | tf_op jit(solution)/shard_map/ppermute | solution.py:36
  22.3 10.4 %collective-permute-start.9 = (bf16[1024,128]{1,0:T(8,128)(2,1)S(1)}, bf16[1024,128]{1,0:T(8,128)(2,1)S(1)}, u32[]{:S(2)}, u32[]{:S(2)}) collective-permute-start(bf16[1024,128]{1,0:T(8,128)(2,1)S(1)} %get-tuple-element.29.refs_1_), channel_id=1, source_target_pairs={{24,0},{0,8},{8,16},{16,24},{25,1},{1,9},{9,17},{17,25},{26,2},{2,... | collective-permute-start | bytes 786440 | tf_op jit(solution)/shard_map/ppermute | solution.py:36
  24.9 7.8 %collective-permute-start.7 = (bf16[1024,128]{1,0:T(8,128)(2,1)S(1)}, bf16[1024,128]{1,0:T(8,128)(2,1)S(1)}, u32[]{:S(2)}, u32[]{:S(2)}) collective-permute-start(bf16[1024,128]{1,0:T(8,128)(2,1)S(1)} %get-tuple-element.29.refs_1_), channel_id=1, source_target_pairs={{8,0},{16,8},{24,16},{0,24},{9,1},{17,9},{25,17},{1,25},{10,2},{18... | collective-permute-start | bytes 786440 | tf_op jit(solution)/shard_map/ppermute | solution.py:36
  32.7 0.7 copy-start
  33.4 24.7 %slice-start = ((s8[6422528]{0:T(1024)(128)(4,1)}), s8[4194304]{0:T(1024)(128)(4,1)S(1)}, s32[]{:S(2)}) async-start(s8[6422528]{0:T(1024)(128)(4,1)} %bitcast.32), calls=%async_computation | async-start | bytes 8388608
  40.0 18.1 %slice-start.1 = ((s8[6422528]{0:T(1024)(128)(4,1)}), s8[2228224]{0:T(1024)(128)(4,1)S(1)}, s32[]{:S(2)}) async-start(s8[6422528]{0:T(1024)(128)(4,1)} %bitcast.32), calls=%async_computation.1 | async-start | bytes 4456448
  40.0 18.1 %collective-permute-start.13 = (bf16[256,1024]{1,0:T(8,128)(2,1)S(1)}, bf16[256,1024]{1,0:T(8,128)(2,1)S(1)}, u32[]{:S(2)}, u32[]{:S(2)}) collective-permute-start(bf16[256,1024]{1,0:T(8,128)(2,1)S(1)} %attend.3), channel_id=1, source_target_pairs={{32,0},{0,32},{33,1},{1,33},{34,2},{2,34},{35,3},{3,35},{36,4},{4,... | collective-permute-start | bytes 1572872 | tf_op jit(solution)/shard_map/ppermute | solution.py:36
  62.5 2.6 %collective-permute-start.14 = (bf16[4,32,3584]{2,1,0:T(8,128)(2,1)S(1)}, bf16[4,32,3584]{2,1,0:T(8,128)(2,1)S(1)}, u32[]{:S(2)}, u32[]{:S(2)}) collective-permute-start(bf16[4,32,3584]{2,1,0:T(8,128)(2,1)S(1)} %get-tuple-element.32), channel_id=1, source_target_pairs={{1,0},{0,1},{3,2},{2,3},{5,4},{4,5},{7,6},{6,7},{9,8},{8,9},{11,10... | collective-permute-start | bytes 2752520 | tf_op jit(solution)/shard_map/ppermute | solution.py:36
  65.5 13.4 %collective-permute-start.15 = (bf16[32,3584]{1,0:T(8,128)(2,1)S(1)}, bf16[32,3584]{1,0:T(8,128)(2,1)S(1)}, u32[]{:S(2)}, u32[]{:S(2)}) collective-permute-start(bf16[32,3584]{1,0:T(8,128)(2,1)S(1)} %pad_maximum_fusion.2), channel_id=1, source_target_pairs={{6,0},{0,2},{2,4},{4,6},{7,1},{1,3},{3,5},{5,7},{14,8},{8,10},{10,... | collective-permute-start | bytes 688136 | tf_op jit(solution)/shard_map/ppermute | solution.py:36
  69.1 14.7 %collective-permute-start.17 = (bf16[32,3584]{1,0:T(8,128)(2,1)S(1)}, bf16[32,3584]{1,0:T(8,128)(2,1)S(1)}, u32[]{:S(2)}, u32[]{:S(2)}) collective-permute-start(bf16[32,3584]{1,0:T(8,128)(2,1)S(1)} %pad_maximum_fusion.3), channel_id=1, source_target_pairs={{2,0},{4,2},{6,4},{0,6},{3,1},{5,3},{7,5},{1,7},{10,8},{12,10},{14... | collective-permute-start | bytes 688136 | tf_op jit(solution)/shard_map/ppermute | solution.py:36
  83.9 8.1 %collective-permute-start.18 = (bf16[16,3584]{1,0:T(8,128)(2,1)S(1)}, bf16[16,3584]{1,0:T(8,128)(2,1)S(1)}, u32[]{:S(2)}, u32[]{:S(2)}) collective-permute-start(bf16[16,3584]{1,0:T(8,128)(2,1)S(1)} %get-tuple-element.33), channel_id=1, source_target_pairs={{2,0},{4,2},{6,4},{0,6},{3,1},{5,3},{7,5},{1,7},{10,8},{12,10},{14... | collective-permute-start | bytes 344072 | tf_op jit(solution)/shard_map/ppermute | solution.py:36
  86.7 8.1 %collective-permute-start.16 = (bf16[16,3584]{1,0:T(8,128)(2,1)S(1)}, bf16[16,3584]{1,0:T(8,128)(2,1)S(1)}, u32[]{:S(2)}, u32[]{:S(2)}) collective-permute-start(bf16[16,3584]{1,0:T(8,128)(2,1)S(1)} %get-tuple-element.34), channel_id=1, source_target_pairs={{6,0},{0,2},{2,4},{4,6},{7,1},{1,3},{3,5},{5,7},{14,8},{8,10},{10,... | collective-permute-start | bytes 344072 | tf_op jit(solution)/shard_map/ppermute | solution.py:36

commit v2 on v1

--- a/solution.py
+++ b/solution.py
@@ -19,6 +19,7 @@
 QUERY_AT = 3 * LIST
 HEAD_AT = QUERY_AT + 16
 TABLE = 256
+W_TILES = 2
 MINUS = -1e30
 SIZES = {"x": 4, "zl": 2, "y": 4, "zh": 4, "core": 2}
 AXES = tuple(SIZES)
@@ -36,7 +37,7 @@
     return lax.ppermute(value, axis, [((i + step) % size, i) for i in range(size)])
 
 
-def table_kernel(order_ref, info_ref, table_ref, inv_ref):
+def table_kernel(order_ref, info_ref, out_ref, table_ref, inv_ref, sem):
     my_x, my_zl, my_y = (lax.axis_index(axis) for axis in CTX)
 
     def invert(block, _):
@@ -75,6 +76,9 @@
         table_ref[i] = 0
         table_ref[LIST + i] = 0
         table_ref[2 * LIST + i] = BLOCKS
+    copy = pltpu.make_async_copy(table_ref, out_ref, sem)
+    copy.start()
+    copy.wait()
 
 
 def make_table(order, info):
@@ -82,16 +86,21 @@
         table_kernel,
         out_shape=jax.ShapeDtypeStruct((TABLE,), jnp.int32),
         in_specs=[SMEM, SMEM],
-        out_specs=SMEM,
-        scratch_shapes=[pltpu.SMEM((BLOCKS,), jnp.int32)],
+        out_specs=ANYWHERE,
+        scratch_shapes=[
+            pltpu.SMEM((TABLE,), jnp.int32),
+            pltpu.SMEM((BLOCKS,), jnp.int32),
+            pltpu.SemaphoreType.DMA,
+        ],
         cost_estimate=pl.CostEstimate(flops=2_000_000_000, bytes_accessed=1000, transcendentals=0),
         name="table",
     )(order, info)
 
 
 def attend_kernel(side, table_hbm, q_hbm, *refs):
-    parts = refs[:8]
-    out_hbm, table_ref, q_ref, out_ref, kv_ref, qs_ref, m_ref, l_ref, acc_ref, kv_sem, in_sem, out_sem = refs[8:]
+    parts, refs = refs[:8], refs[8:]
+    out_hbm, *refs = refs
+    table_ref, q_ref, out_ref, kv_ref, qs_ref, m_ref, l_ref, acc_ref, kv_sem, in_sem, out_sem = refs
     part_rows = parts[0].shape[0]
     half = 4 * part_rows
     table_copy = pltpu.make_async_copy(table_hbm, table_ref, in_sem.at[0])
@@ -216,9 +225,9 @@
     rows = GROUP * BLK
     return pl.pallas_call(
         functools.partial(attend_kernel, side),
-        out_shape=jax.ShapeDtypeStruct((ROWS, FEATS + BLK), jnp.bfloat16),
+        out_shape=(jax.ShapeDtypeStruct((ROWS, FEATS + BLK), jnp.bfloat16),),
         in_specs=[ANYWHERE] * 10,
-        out_specs=ANYWHERE,
+        out_specs=(ANYWHERE,),
         scratch_shapes=[
             pltpu.SMEM((TABLE,), jnp.int32),
             pltpu.VMEM(q.shape, jnp.bfloat16),
@@ -232,57 +241,57 @@
             pltpu.SemaphoreType.DMA((2,)),
             pltpu.SemaphoreType.DMA((2,)),
         ],
-        compiler_params=pltpu.CompilerParams(vmem_limit_bytes=40 * 1024 * 1024),
+        compiler_params=pltpu.CompilerParams(vmem_limit_bytes=32 * 1024 * 1024),
         cost_estimate=pl.CostEstimate(flops=4_000_000_000, bytes_accessed=3_000_000, transcendentals=4_000_000),
         name="attend",
     )(table, q, *parts)
 
 
-def project_kernel(table_ref, a_ref, b_ref, w_ref, keep_ref, send_ref, att_ref):
+def project_kernel(table_hbm, a_hbm, b_hbm, w_ref, keep_ref, send_ref, table_ref, a_ref, b_ref, att_ref, in_sem):
+    tile = w_ref.shape[1] // W_TILES
+    in_copies = [
+        pltpu.make_async_copy(source, target, in_sem.at[i])
+        for i, (source, target) in enumerate(((table_hbm, table_ref), (a_hbm, a_ref), (b_hbm, b_ref)))
+    ]
+    for copy in in_copies:
+        copy.start()
+    for copy in in_copies:
+        copy.wait()
     my_zh, my_core = table_ref[HEAD_AT], table_ref[HEAD_AT + 1]
-
-    @pl.when(pl.program_id(0) == 0)
-    def _():
-        stats_a = a_ref[:, FEATS:].astype(jnp.float32)
-        stats_b = b_ref[:, FEATS:].astype(jnp.float32)
-        for h in range(GROUP):
-
-            def level(stats):
-                return stats[:, h : h + 1] + stats[:, 8 + h : 9 + h] + stats[:, 16 + h : 17 + h]
-
-            weight_a = 1.0 / (1.0 + jnp.exp2(level(stats_b) - level(stats_a)))
-            cols = slice(h * HD, (h + 1) * HD)
-            a, b = a_ref[:, cols].astype(jnp.float32), b_ref[:, cols].astype(jnp.float32)
-            att_ref[:, cols] = (b + (a - b) * weight_a).astype(jnp.bfloat16)
-
-    tile = keep_ref.shape[2]
-    cols = pl.ds(pl.multiple_of(pl.program_id(0) * tile, tile), tile)
-    res = jnp.dot(att_ref[...], w_ref[:, cols], preferred_element_type=jnp.float32).astype(jnp.bfloat16)
-    for z in range(4):
-        to = (z - my_zh) & 3
-        zero, one = res[z * 64 : z * 64 + 32, :], res[z * 64 + 32 : z * 64 + 64, :]
-        keep_ref[to] = jnp.where(my_core == 0, zero, one)
-        send_ref[to] = jnp.where(my_core == 0, one, zero)
+    stats_a = a_ref[:, FEATS:].astype(jnp.float32)
+    stats_b = b_ref[:, FEATS:].astype(jnp.float32)
+    gap = stats_b - stats_a
+    for h in range(GROUP):
+        levels = gap[:, h : h + 1] + gap[:, 8 + h : 9 + h] + gap[:, 16 + h : 17 + h]
+        weight_a = 1.0 / (1.0 + jnp.exp2(jnp.broadcast_to(levels, (ROWS, HD))))
+        cols = slice(h * HD, (h + 1) * HD)
+        a, b = a_ref[:, cols].astype(jnp.float32), b_ref[:, cols].astype(jnp.float32)
+        att_ref[:, cols] = (b + (a - b) * weight_a).astype(jnp.bfloat16)
+    for i in range(W_TILES):
+        cols = slice(i * tile, (i + 1) * tile)
+        res = jnp.dot(att_ref[...], w_ref[:, cols], preferred_element_type=jnp.float32).astype(jnp.bfloat16)
+        for z in range(4):
+            to = (z - my_zh) & 3
+            zero, one = res[z * 64 : z * 64 + 32, :], res[z * 64 + 32 : z * 64 + 64, :]
+            keep_ref[to, :, cols] = jnp.where(my_core == 0, zero, one)
+            send_ref[to, :, cols] = jnp.where(my_core == 0, one, zero)
 
 
 def project(table, a, b, w):
-    out_cols = w.shape[1]
-    tile = 512
-    piece = jax.ShapeDtypeStruct((4, 32, out_cols), jnp.bfloat16)
-    out_spec = pl.BlockSpec((4, 32, tile), lambda i: (0, 0, i))
+    piece = jax.ShapeDtypeStruct((4, 32, w.shape[1]), jnp.bfloat16)
     return pl.pallas_call(
         project_kernel,
-        grid=(out_cols // tile,),
         out_shape=(piece, piece),
-        in_specs=[
-            SMEM,
-            pl.BlockSpec(a.shape, lambda i: (0, 0)),
-            pl.BlockSpec(b.shape, lambda i: (0, 0)),
-            pl.BlockSpec(w.shape, lambda i: (0, 0)),
+        in_specs=[ANYWHERE] * 3 + [VMEM],
+        out_specs=(VMEM, VMEM),
+        scratch_shapes=[
+            pltpu.SMEM((TABLE,), jnp.int32),
+            pltpu.VMEM(a.shape, jnp.bfloat16),
+            pltpu.VMEM(b.shape, jnp.bfloat16),
+            pltpu.VMEM((ROWS, FEATS), jnp.bfloat16),
+            pltpu.SemaphoreType.DMA((3,)),
         ],
-        out_specs=(out_spec, out_spec),
-        scratch_shapes=[pltpu.VMEM((ROWS, FEATS), jnp.bfloat16)],
-        compiler_params=pltpu.CompilerParams(vmem_limit_bytes=24 * 1024 * 1024),
+        compiler_params=pltpu.CompilerParams(vmem_limit_bytes=20 * 1024 * 1024),
         cost_estimate=pl.CostEstimate(flops=1_640_000_000, bytes_accessed=9_000_000, transcendentals=1792),
         name="project",
     )(table, a, b, w)
@@ -301,10 +310,10 @@
     k, v = lax.optimization_barrier((k, v))
     parts = [k, v]
     for o in OFFSETS[1:]:
-        parts += [shift(v, "y", o), shift(k, "x", o)]
-    other = attend(0, table, other_q, parts)
+        parts += lax.optimization_barrier((shift(v, "y", o), shift(k, "x", o)))
+    (other,) = attend(0, table, other_q, parts)
     back = shift(other, "zl", 1)
-    own = attend(1, table, q, parts)
+    (own,) = attend(1, table, q, parts)
     keep, send = project(table, own, back, out_weight)
     pieces = keep.astype(jnp.float32) + shift(send, "core", 1).astype(jnp.float32)
     low = pieces.astype(jnp.bfloat16)

time: 93.8 us -> 90.5 us (0.965)
  the two profiles are of different devices: /device:TPU:16 before, /device:TPU:32 now
where the time goes in v2:
time: 90.5 us; the launch traced here: 90.9 us
  starting transfers between devices  35.9 us (40%)
  waiting for transfers between devices  29 us (32%)
  Pallas kernels  23.9 us (26%)
  other arithmetic  1.18 us (1%)
    ppermute x19, starting transfers between devices, shift(): lax.ppermute(value, axis, [((i + step) % size, i) for i in range(size)])  35.9 us
    ppermute x19, waiting for transfers between devices, shift(): lax.ppermute(value, axis, [((i + step) % size, i) for i in range(size)])  29 us
    pallas_call x2, Pallas kernels, attend(): pl.pallas_call(functools.partial(attend_kernel, side), out_shape=(jax.Sha...  17.7 us
    pallas_call x1, Pallas kernels, project(): pl.pallas_call(project_kernel, out_shape=(piece, piece), in_specs=[ANYWHE...  3.09 us
    pallas_call x1, Pallas kernels, make_table(): pl.pallas_call(table_kernel, out_shape=jax.ShapeDtypeStruct((TABLE,), jnp...  3.06 us
  transfers between devices with their start and end apart: 19, of which 10 were waited for; matrix products, arithmetic and copies ran while one was open for 0% of the time, Pallas kernels for 16%

profile of v2, /device:TPU:32, one launch (start us, length us, event | category | flops | bytes accessed | tf_op | source)
XLA Modules:
  0.0 90.9 jit_solution(2876634285963080908)
XLA Ops:
  0.0 1.8 %collective-permute-start.6 = (bf16[7,256,128]{2,1,0:T(8,128)(2,1)}, bf16[7,256,128]{2,1,0:T(8,128)(2,1)S(1)}, u32[]{:S(2)}, u32[]{:S(2)}) collective-permute-start(bf16[7,256,128]{2,1,0:T(8,128)(2,1)} %bitcast.34), channel_id=1, source_target_pairs={{32,0},{0,32},{33,1},{1,33},{34,2},{2,34},{35,3},{3,35},{36,4},{4,... | collective-permute-start | bytes 1376264 | tf_op jit(solution)/shard_map/ppermute | solution.py:37
  1.8 1.5 %collective-permute-start.2 = (bf16[256,128]{1,0:T(8,128)(2,1)}, bf16[256,128]{1,0:T(8,128)(2,1)S(1)}, u32[]{:S(2)}, u32[]{:S(2)}) collective-permute-start(bf16[256,128]{1,0:T(8,128)(2,1)} %bitcast.36), channel_id=1, source_target_pairs={{16,0},{24,8},{0,16},{8,24},{17,1},{25,9},{1,17},{9,25},{18,2},{26... | collective-permute-start | bytes 196616 | tf_op jit(solution)/shard_map/ppermute | solution.py:37
  3.3 0.7 collective-permute-start.1
  4.0 2.6 %collective-permute-start = (bf16[256,128]{1,0:T(8,128)(2,1)}, bf16[256,128]{1,0:T(8,128)(2,1)S(1)}, u32[]{:S(2)}, u32[]{:S(2)}) collective-permute-start(bf16[256,128]{1,0:T(8,128)(2,1)} %bitcast.38), channel_id=1, source_target_pairs={{8,0},{16,8},{24,16},{0,24},{9,1},{17,9},{25,17},{1,25},{10,2},{18... | collective-permute-start | bytes 196616 | tf_op jit(solution)/shard_map/ppermute | solution.py:37
  6.5 3.0 %collective-permute-start.5 = (bf16[256,128]{1,0:T(8,128)(2,1)}, bf16[256,128]{1,0:T(8,128)(2,1)S(1)}, u32[]{:S(2)}, u32[]{:S(2)}) collective-permute-start(bf16[256,128]{1,0:T(8,128)(2,1)} %bitcast.40), channel_id=1, source_target_pairs={{128,0},{192,64},{0,128},{64,192},{129,1},{193,65},{1,129},{65,193... | collective-permute-start | bytes 196616 | tf_op jit(solution)/shard_map/ppermute | solution.py:37
  9.6 0.6 collective-permute-start.4
  10.2 2.6 %collective-permute-start.3 = (bf16[256,128]{1,0:T(8,128)(2,1)}, bf16[256,128]{1,0:T(8,128)(2,1)S(1)}, u32[]{:S(2)}, u32[]{:S(2)}) collective-permute-start(bf16[256,128]{1,0:T(8,128)(2,1)} %bitcast.42), channel_id=1, source_target_pairs={{64,0},{128,64},{192,128},{0,192},{65,1},{129,65},{193,129},{1,193... | collective-permute-start | bytes 196616 | tf_op jit(solution)/shard_map/ppermute | solution.py:37
  12.8 3.1 %table.1.table_hbm = s32[256]{0:T(256)} custom-call(s32[64]{0:T(128)} %order_ref.1, s32[3,64]{1,0:T(4,128)} %bitcast.44), custom_call_target="tpu_custom_call" | custom-call | flops 2000000000 | bytes 1000 | tf_op jit(solution)/shard_map/table/pallas_call | solution.py:85
  16.0 0.9 collective-permute-start.12
  16.9 1.9 %collective-permute-start.11 = (bf16[1024,128]{1,0:T(8,128)(2,1)S(1)}, bf16[1024,128]{1,0:T(8,128)(2,1)S(1)}, u32[]{:S(2)}, u32[]{:S(2)}) collective-permute-start(bf16[1024,128]{1,0:T(8,128)(2,1)S(1)} %get-tuple-element.35.refs_1_), channel_id=1, source_target_pairs={{16,0},{24,8},{0,16},{8,24},{17,1},{25,9},{1,17},{9,25},{18,2},{26... | collective-permute-start | bytes 786440 | tf_op jit(solution)/shard_map/ppermute | solution.py:37
  18.8 0.7 collective-permute-start.10
  19.5 0.9 collective-permute-start.9
  20.4 2.4 %collective-permute-start.8 = (bf16[1024,128]{1,0:T(8,128)(2,1)S(1)}, bf16[1024,128]{1,0:T(8,128)(2,1)S(1)}, u32[]{:S(2)}, u32[]{:S(2)}) collective-permute-start(bf16[1024,128]{1,0:T(8,128)(2,1)S(1)} %get-tuple-element.34.refs_0_), channel_id=1, source_target_pairs={{64,0},{128,64},{192,128},{0,192},{65,1},{129,65},{193,129},{1,193... | collective-permute-start | bytes 786440 | tf_op jit(solution)/shard_map/ppermute | solution.py:37
  22.7 3.9 %collective-permute-done.12.refs_7_ = bf16[1024,128]{1,0:T(8,128)(2,1)S(1)} collective-permute-done((bf16[1024,128]{1,0:T(8,128)(2,1)S(1)}, bf16[1024,128]{1,0:T(8,128)(2,1)S(1)}, u32[]{:S(2)}, u32[]{:S(2)}) %collective-permute-start.12) | collective-permute-done | bytes 262176 | tf_op jit(solution)/shard_map/ppermute | solution.py:37
  27.4 2.1 %collective-permute-done.10.refs_5_ = bf16[1024,128]{1,0:T(8,128)(2,1)S(1)} collective-permute-done((bf16[1024,128]{1,0:T(8,128)(2,1)S(1)}, bf16[1024,128]{1,0:T(8,128)(2,1)S(1)}, u32[]{:S(2)}, u32[]{:S(2)}) %collective-permute-start.10) | collective-permute-done | bytes 262176 | tf_op jit(solution)/shard_map/ppermute | solution.py:37
  29.5 0.7 collective-permute-done.9.refs_4_
  30.2 2.9 %collective-permute-done.7.refs_2_ = bf16[1024,128]{1,0:T(8,128)(2,1)S(1)} collective-permute-done((bf16[1024,128]{1,0:T(8,128)(2,1)S(1)}, bf16[1024,128]{1,0:T(8,128)(2,1)S(1)}, u32[]{:S(2)}, u32[]{:S(2)}) %collective-permute-start.7) | collective-permute-done | bytes 262176 | tf_op jit(solution)/shard_map/ppermute | solution.py:37
  33.1 0.7 copy-done
  33.7 6.6 %attend.3 = bf16[256,1024]{1,0:T(8,128)(2,1)S(1)} custom-call(s32[256]{0:T(256)S(1)} %copy-done, bf16[7,256,128]{2,1,0:T(8,128)(2,1)S(1)} %collective-permute-done.6.q_hbm, bf16[1024,128]{1,0:T(8,128)(2,1)S(1)} %get-tuple-element.34.refs_0_, bf16[1024,128]{1,0:T(8,128)(2,1)S(1)} %get-tuple-element.35.refs_1_, ...), custom_call_target="tpu_custom_call" | custom-call | flops 4000000000 | bytes 3000000 | tf_op jit(solution)/shard_map/attend/pallas_call | solution.py:226
  40.4 7.3 %collective-permute-start.13 = (bf16[256,1024]{1,0:T(8,128)(2,1)S(1)}, bf16[256,1024]{1,0:T(8,128)(2,1)S(1)}, u32[]{:S(2)}, u32[]{:S(2)}) collective-permute-start(bf16[256,1024]{1,0:T(8,128)(2,1)S(1)} %attend.3), channel_id=1, source_target_pairs={{32,0},{0,32},{33,1},{1,33},{34,2},{2,34},{35,3},{3,35},{36,4},{4,... | collective-permute-start | bytes 1572872 | tf_op jit(solution)/shard_map/ppermute | solution.py:37
  47.6 11.1 %attend.2.a_hbm = bf16[256,1024]{1,0:T(8,128)(2,1)S(1)} custom-call(s32[256]{0:T(256)S(1)} %copy-done, bf16[7,256,128]{2,1,0:T(8,128)(2,1)S(1)} %bitcast.35, bf16[1024,128]{1,0:T(8,128)(2,1)S(1)} %get-tuple-element.34.refs_0_, bf16[1024,128]{1,0:T(8,128)(2,1)S(1)} %get-tuple-element.35.refs_1_, bf16[1024,128]{1,0:T(8,128)(2,1)S(1)} %collective-permute-done.7.refs_2_, ...), custom_call_target="tpu_custom_call" | custom-call | flops 4000000000 | bytes 3000000 | tf_op jit(solution)/shard_map/attend/pallas_call | solution.py:226
  58.8 3.1 %project.1 = (bf16[4,32,3584]{2,1,0:T(8,128)(2,1)S(1)}, bf16[4,32,3584]{2,1,0:T(8,128)(2,1)S(1)}) custom-call(s32[256]{0:T(256)S(1)} %copy-done, bf16[256,1024]{1,0:T(8,128)(2,1)S(1)} %attend.2.a_hbm, bf16[256,1024]{1,0:T(8,128)(2,1)S(1)} %collective-permute-done.13.b_hbm, bf16[896,3584]{1,0:T(8,128)(2,1)S(1)} %bitcast.33), custom_call_target="tpu_custom_call" | custom-call | flops 1640000000 | bytes 9000000 | tf_op jit(solution)/shard_map/project/pallas_call | solution.py:282
  62.2 2.5 %collective-permute-done.14 = bf16[4,32,3584]{2,1,0:T(8,128)(2,1)S(1)} collective-permute-done((bf16[4,32,3584]{2,1,0:T(8,128)(2,1)S(1)}, bf16[4,32,3584]{2,1,0:T(8,128)(2,1)S(1)}, u32[]{:S(2)}, u32[]{:S(2)}) %collective-permute-start.14) | collective-permute-done | bytes 917536 | tf_op jit(solution)/shard_map/ppermute | solution.py:37
  65.1 3.3 %collective-permute-start.15 = (bf16[32,3584]{1,0:T(8,128)(2,1)S(1)}, bf16[32,3584]{1,0:T(8,128)(2,1)S(1)}, u32[]{:S(2)}, u32[]{:S(2)}) collective-permute-start(bf16[32,3584]{1,0:T(8,128)(2,1)S(1)} %pad_maximum_fusion.2), channel_id=1, source_target_pairs={{6,0},{0,2},{2,4},{4,6},{7,1},{1,3},{3,5},{5,7},{14,8},{8,10},{10,... | collective-permute-start | bytes 688136 | tf_op jit(solution)/shard_map/ppermute | solution.py:37
  68.4 2.2 %collective-permute-start.17 = (bf16[32,3584]{1,0:T(8,128)(2,1)S(1)}, bf16[32,3584]{1,0:T(8,128)(2,1)S(1)}, u32[]{:S(2)}, u32[]{:S(2)}) collective-permute-start(bf16[32,3584]{1,0:T(8,128)(2,1)S(1)} %pad_maximum_fusion.3), channel_id=1, source_target_pairs={{2,0},{4,2},{6,4},{0,6},{3,1},{5,3},{7,5},{1,7},{10,8},{12,10},{14... | collective-permute-start | bytes 688136 | tf_op jit(solution)/shard_map/ppermute | solution.py:37
  70.7 8.2 %collective-permute-done.15 = bf16[32,3584]{1,0:T(8,128)(2,1)S(1)} collective-permute-done((bf16[32,3584]{1,0:T(8,128)(2,1)S(1)}, bf16[32,3584]{1,0:T(8,128)(2,1)S(1)}, u32[]{:S(2)}, u32[]{:S(2)}) %collective-permute-start.15) | collective-permute-done | bytes 229408 | tf_op jit(solution)/shard_map/ppermute | solution.py:37
  78.9 3.5 %collective-permute-done.17 = bf16[32,3584]{1,0:T(8,128)(2,1)S(1)} collective-permute-done((bf16[32,3584]{1,0:T(8,128)(2,1)S(1)}, bf16[32,3584]{1,0:T(8,128)(2,1)S(1)}, u32[]{:S(2)}, u32[]{:S(2)}) %collective-permute-start.17) | collective-permute-done | bytes 229408 | tf_op jit(solution)/shard_map/ppermute | solution.py:37
  82.5 0.6 collective-permute-start.18
  83.1 2.4 %collective-permute-start.16 = (bf16[16,3584]{1,0:T(8,128)(2,1)S(1)}, bf16[16,3584]{1,0:T(8,128)(2,1)S(1)}, u32[]{:S(2)}, u32[]{:S(2)}) collective-permute-start(bf16[16,3584]{1,0:T(8,128)(2,1)S(1)} %get-tuple-element.46), channel_id=1, source_target_pairs={{6,0},{0,2},{2,4},{4,6},{7,1},{1,3},{3,5},{5,7},{14,8},{8,10},{10,... | collective-permute-start | bytes 344072 | tf_op jit(solution)/shard_map/ppermute | solution.py:37
  85.5 3.0 %collective-permute-done.18 = bf16[16,3584]{1,0:T(8,128)(2,1)S(1)} collective-permute-done((bf16[16,3584]{1,0:T(8,128)(2,1)S(1)}, bf16[16,3584]{1,0:T(8,128)(2,1)S(1)}, u32[]{:S(2)}, u32[]{:S(2)}) %collective-permute-start.18) | collective-permute-done | bytes 114720 | tf_op jit(solution)/shard_map/ppermute | solution.py:37
  88.6 1.5 %collective-permute-done.16 = bf16[16,3584]{1,0:T(8,128)(2,1)S(1)} collective-permute-done((bf16[16,3584]{1,0:T(8,128)(2,1)S(1)}, bf16[16,3584]{1,0:T(8,128)(2,1)S(1)}, u32[]{:S(2)}, u32[]{:S(2)}) %collective-permute-start.16) | collective-permute-done | bytes 114720 | tf_op jit(solution)/shard_map/ppermute | solution.py:37
  90.1 0.8 fusion.2
  (32 shorter events, 1.6 us)
Async XLA Ops:
  0.0 15.9 %collective-permute-start.6 = (bf16[7,256,128]{2,1,0:T(8,128)(2,1)}, bf16[7,256,128]{2,1,0:T(8,128)(2,1)S(1)}, u32[]{:S(2)}, u32[]{:S(2)}) collective-permute-start(bf16[7,256,128]{2,1,0:T(8,128)(2,1)} %bitcast.34), channel_id=1, source_target_pairs={{32,0},{0,32},{33,1},{1,33},{34,2},{2,34},{35,3},{3,35},{36,4},{4,... | collective-permute-start | bytes 1376264 | tf_op jit(solution)/shard_map/ppermute | solution.py:37
  1.8 7.7 %collective-permute-start.2 = (bf16[256,128]{1,0:T(8,128)(2,1)}, bf16[256,128]{1,0:T(8,128)(2,1)S(1)}, u32[]{:S(2)}, u32[]{:S(2)}) collective-permute-start(bf16[256,128]{1,0:T(8,128)(2,1)} %bitcast.36), channel_id=1, source_target_pairs={{16,0},{24,8},{0,16},{8,24},{17,1},{25,9},{1,17},{9,25},{18,2},{26... | collective-permute-start | bytes 196616 | tf_op jit(solution)/shard_map/ppermute | solution.py:37
  3.3 6.9 %collective-permute-start.1 = (bf16[256,128]{1,0:T(8,128)(2,1)}, bf16[256,128]{1,0:T(8,128)(2,1)S(1)}, u32[]{:S(2)}, u32[]{:S(2)}) collective-permute-start(bf16[256,128]{1,0:T(8,128)(2,1)} %bitcast.37), channel_id=1, source_target_pairs={{24,0},{0,8},{8,16},{16,24},{25,1},{1,9},{9,17},{17,25},{26,2},{2,... | collective-permute-start | bytes 196616 | tf_op jit(solution)/shard_map/ppermute | solution.py:37
  4.0 11.9 %collective-permute-start = (bf16[256,128]{1,0:T(8,128)(2,1)}, bf16[256,128]{1,0:T(8,128)(2,1)S(1)}, u32[]{:S(2)}, u32[]{:S(2)}) collective-permute-start(bf16[256,128]{1,0:T(8,128)(2,1)} %bitcast.38), channel_id=1, source_target_pairs={{8,0},{16,8},{24,16},{0,24},{9,1},{17,9},{25,17},{1,25},{10,2},{18... | collective-permute-start | bytes 196616 | tf_op jit(solution)/shard_map/ppermute | solution.py:37
  6.5 9.4 %collective-permute-start.5 = (bf16[256,128]{1,0:T(8,128)(2,1)}, bf16[256,128]{1,0:T(8,128)(2,1)S(1)}, u32[]{:S(2)}, u32[]{:S(2)}) collective-permute-start(bf16[256,128]{1,0:T(8,128)(2,1)} %bitcast.40), channel_id=1, source_target_pairs={{128,0},{192,64},{0,128},{64,192},{129,1},{193,65},{1,129},{65,193... | collective-permute-start | bytes 196616 | tf_op jit(solution)/shard_map/ppermute | solution.py:37
  9.6 6.3 %collective-permute-start.4 = (bf16[256,128]{1,0:T(8,128)(2,1)}, bf16[256,128]{1,0:T(8,128)(2,1)S(1)}, u32[]{:S(2)}, u32[]{:S(2)}) collective-permute-start(bf16[256,128]{1,0:T(8,128)(2,1)} %bitcast.41), channel_id=1, source_target_pairs={{192,0},{0,64},{64,128},{128,192},{193,1},{1,65},{65,129},{129,193... | collective-permute-start | bytes 196616 | tf_op jit(solution)/shard_map/ppermute | solution.py:37
  10.2 5.8 %collective-permute-start.3 = (bf16[256,128]{1,0:T(8,128)(2,1)}, bf16[256,128]{1,0:T(8,128)(2,1)S(1)}, u32[]{:S(2)}, u32[]{:S(2)}) collective-permute-start(bf16[256,128]{1,0:T(8,128)(2,1)} %bitcast.42), channel_id=1, source_target_pairs={{64,0},{128,64},{192,128},{0,192},{65,1},{129,65},{193,129},{1,193... | collective-permute-start | bytes 196616 | tf_op jit(solution)/shard_map/ppermute | solution.py:37
  12.8 3.1 %copy-start.2 = (bf16[256,1,128]{2,0,1:T(8,128)(2,1)S(1)}, bf16[256,1,128]{2,0,1:T(8,128)(2,1)}, u32[]{:S(2)}) copy-start(bf16[256,1,128]{2,0,1:T(8,128)(2,1)} %param.7) | copy-start | bytes 196612
  12.8 3.1 %copy-start.3 = (bf16[256,1,128]{2,0,1:T(8,128)(2,1)S(1)}, bf16[256,1,128]{2,0,1:T(8,128)(2,1)}, u32[]{:S(2)}) copy-start(bf16[256,1,128]{2,0,1:T(8,128)(2,1)} %param.8) | copy-start | bytes 196612
  16.0 31.7 %copy-start.1 = (bf16[256,7,128]{2,0,1:T(8,128)(2,1)S(1)}, bf16[256,7,128]{2,0,1:T(8,128)(2,1)}, u32[]{:S(2)}) copy-start(bf16[256,7,128]{2,0,1:T(8,128)(2,1)} %param.6) | copy-start | bytes 1376260
  16.0 10.7 %collective-permute-start.12 = (bf16[1024,128]{1,0:T(8,128)(2,1)S(1)}, bf16[1024,128]{1,0:T(8,128)(2,1)S(1)}, u32[]{:S(2)}, u32[]{:S(2)}) collective-permute-start(bf16[1024,128]{1,0:T(8,128)(2,1)S(1)} %get-tuple-element.34.refs_0_), channel_id=1, source_target_pairs={{128,0},{192,64},{0,128},{64,192},{129,1},{193,65},{1,129},{65,193... | collective-permute-start | bytes 786440 | tf_op jit(solution)/shard_map/ppermute | solution.py:37
  16.9 10.5 %collective-permute-start.11 = (bf16[1024,128]{1,0:T(8,128)(2,1)S(1)}, bf16[1024,128]{1,0:T(8,128)(2,1)S(1)}, u32[]{:S(2)}, u32[]{:S(2)}) collective-permute-start(bf16[1024,128]{1,0:T(8,128)(2,1)S(1)} %get-tuple-element.35.refs_1_), channel_id=1, source_target_pairs={{16,0},{24,8},{0,16},{8,24},{17,1},{25,9},{1,17},{9,25},{18,2},{26... | collective-permute-start | bytes 786440 | tf_op jit(solution)/shard_map/ppermute | solution.py:37
  18.8 10.7 %collective-permute-start.10 = (bf16[1024,128]{1,0:T(8,128)(2,1)S(1)}, bf16[1024,128]{1,0:T(8,128)(2,1)S(1)}, u32[]{:S(2)}, u32[]{:S(2)}) collective-permute-start(bf16[1024,128]{1,0:T(8,128)(2,1)S(1)} %get-tuple-element.34.refs_0_), channel_id=1, source_target_pairs={{192,0},{0,64},{64,128},{128,192},{193,1},{1,65},{65,129},{129,193... | collective-permute-start | bytes 786440 | tf_op jit(solution)/shard_map/ppermute | solution.py:37
  19.5 10.7 %collective-permute-start.9 = (bf16[1024,128]{1,0:T(8,128)(2,1)S(1)}, bf16[1024,128]{1,0:T(8,128)(2,1)S(1)}, u32[]{:S(2)}, u32[]{:S(2)}) collective-permute-start(bf16[1024,128]{1,0:T(8,128)(2,1)S(1)} %get-tuple-element.35.refs_1_), channel_id=1, source_target_pairs={{24,0},{0,8},{8,16},{16,24},{25,1},{1,9},{9,17},{17,25},{26,2},{2,... | collective-permute-start | bytes 786440 | tf_op jit(solution)/shard_map/ppermute | solution.py:37
  20.4 9.8 %collective-permute-start.8 = (bf16[1024,128]{1,0:T(8,128)(2,1)S(1)}, bf16[1024,128]{1,0:T(8,128)(2,1)S(1)}, u32[]{:S(2)}, u32[]{:S(2)}) collective-permute-start(bf16[1024,128]{1,0:T(8,128)(2,1)S(1)} %get-tuple-element.34.refs_0_), channel_id=1, source_target_pairs={{64,0},{128,64},{192,128},{0,192},{65,1},{129,65},{193,129},{1,193... | collective-permute-start | bytes 786440 | tf_op jit(solution)/shard_map/ppermute | solution.py:37
  26.7 6.4 %collective-permute-start.7 = (bf16[1024,128]{1,0:T(8,128)(2,1)S(1)}, bf16[1024,128]{1,0:T(8,128)(2,1)S(1)}, u32[]{:S(2)}, u32[]{:S(2)}) collective-permute-start(bf16[1024,128]{1,0:T(8,128)(2,1)S(1)} %get-tuple-element.35.refs_1_), channel_id=1, source_target_pairs={{8,0},{16,8},{24,16},{0,24},{9,1},{17,9},{25,17},{1,25},{10,2},{18... | collective-permute-start | bytes 786440 | tf_op jit(solution)/shard_map/ppermute | solution.py:37
  33.1 0.7 copy-start
  33.7 25.0 %slice-start = ((s8[6422528]{0:T(1024)(128)(4,1)}), s8[4194304]{0:T(1024)(128)(4,1)S(1)}, s32[]{:S(2)}) async-start(s8[6422528]{0:T(1024)(128)(4,1)} %bitcast.32), calls=%async_computation | async-start | bytes 8388608
  40.3 18.4 %slice-start.1 = ((s8[6422528]{0:T(1024)(128)(4,1)}), s8[2228224]{0:T(1024)(128)(4,1)S(1)}, s32[]{:S(2)}) async-start(s8[6422528]{0:T(1024)(128)(4,1)} %bitcast.32), calls=%async_computation.1 | async-start | bytes 4456448
  40.4 18.4 %collective-permute-start.13 = (bf16[256,1024]{1,0:T(8,128)(2,1)S(1)}, bf16[256,1024]{1,0:T(8,128)(2,1)S(1)}, u32[]{:S(2)}, u32[]{:S(2)}) collective-permute-start(bf16[256,1024]{1,0:T(8,128)(2,1)S(1)} %attend.3), channel_id=1, source_target_pairs={{32,0},{0,32},{33,1},{1,33},{34,2},{2,34},{35,3},{3,35},{36,4},{4,... | collective-permute-start | bytes 1572872 | tf_op jit(solution)/shard_map/ppermute | solution.py:37
  61.9 2.8 %collective-permute-start.14 = (bf16[4,32,3584]{2,1,0:T(8,128)(2,1)S(1)}, bf16[4,32,3584]{2,1,0:T(8,128)(2,1)S(1)}, u32[]{:S(2)}, u32[]{:S(2)}) collective-permute-start(bf16[4,32,3584]{2,1,0:T(8,128)(2,1)S(1)} %get-tuple-element.44), channel_id=1, source_target_pairs={{1,0},{0,1},{3,2},{2,3},{5,4},{4,5},{7,6},{6,7},{9,8},{8,9},{11,10... | collective-permute-start | bytes 2752520 | tf_op jit(solution)/shard_map/ppermute | solution.py:37
  65.1 13.8 %collective-permute-start.15 = (bf16[32,3584]{1,0:T(8,128)(2,1)S(1)}, bf16[32,3584]{1,0:T(8,128)(2,1)S(1)}, u32[]{:S(2)}, u32[]{:S(2)}) collective-permute-start(bf16[32,3584]{1,0:T(8,128)(2,1)S(1)} %pad_maximum_fusion.2), channel_id=1, source_target_pairs={{6,0},{0,2},{2,4},{4,6},{7,1},{1,3},{3,5},{5,7},{14,8},{8,10},{10,... | collective-permute-start | bytes 688136 | tf_op jit(solution)/shard_map/ppermute | solution.py:37
  68.4 14.0 %collective-permute-start.17 = (bf16[32,3584]{1,0:T(8,128)(2,1)S(1)}, bf16[32,3584]{1,0:T(8,128)(2,1)S(1)}, u32[]{:S(2)}, u32[]{:S(2)}) collective-permute-start(bf16[32,3584]{1,0:T(8,128)(2,1)S(1)} %pad_maximum_fusion.3), channel_id=1, source_target_pairs={{2,0},{4,2},{6,4},{0,6},{3,1},{5,3},{7,5},{1,7},{10,8},{12,10},{14... | collective-permute-start | bytes 688136 | tf_op jit(solution)/shard_map/ppermute | solution.py:37
  82.5 6.1 %collective-permute-start.18 = (bf16[16,3584]{1,0:T(8,128)(2,1)S(1)}, bf16[16,3584]{1,0:T(8,128)(2,1)S(1)}, u32[]{:S(2)}, u32[]{:S(2)}) collective-permute-start(bf16[16,3584]{1,0:T(8,128)(2,1)S(1)} %get-tuple-element.45), channel_id=1, source_target_pairs={{2,0},{4,2},{6,4},{0,6},{3,1},{5,3},{7,5},{1,7},{10,8},{12,10},{14... | collective-permute-start | bytes 344072 | tf_op jit(solution)/shard_map/ppermute | solution.py:37
  83.1 7.0 %collective-permute-start.16 = (bf16[16,3584]{1,0:T(8,128)(2,1)S(1)}, bf16[16,3584]{1,0:T(8,128)(2,1)S(1)}, u32[]{:S(2)}, u32[]{:S(2)}) collective-permute-start(bf16[16,3584]{1,0:T(8,128)(2,1)S(1)} %get-tuple-element.46), channel_id=1, source_target_pairs={{6,0},{0,2},{2,4},{4,6},{7,1},{1,3},{3,5},{5,7},{14,8},{8,10},{10,... | collective-permute-start | bytes 344072 | tf_op jit(solution)/shard_map/ppermute | solution.py:37
